TPU v7x, 256 devices: a whole 4x4x8 slice. The times are simulated.
256 devices in a mesh: section: 4 (over x), coil: 32 (over y, z), cuts: 2 (over core).
Axes of the slice: x: 4, y: 4, z: 8, core: 2. Of those that a mesh axis runs over, the one named last changes fastest.
Arguments:
- initial: bfloat16 [2, 32, 80, 2, 128], P(None, 'coil', 'cuts'), may hold values from -6 to 6
- sens: bfloat16 [2, 64, 32, 80, 2, 128], P(None, ('coil', 'cuts')), may hold values from -3.5 to 3.5
- kspace: bfloat16 [2, 64, 32, 80, 2, 128], P(None, ('coil', 'cuts')), may hold values from -6 to 6
- mask: int32 [2, 80, 128], replicated, may hold values 0 or 1
- step_sizes: float32 [4], P('section'), may hold values from 0.3 to 1.5
- conv_in: bfloat16 [4, 128, 18], P('section'), may hold values from -1.5 to 1.5
- bias_in: float32 [4, 128], P('section'), may hold values from -3 to 3
- conv_out: bfloat16 [4, 18, 128], P('section'), may hold values from -0.1875 to 0.1875
Outputs:
- cascade_images: bfloat16 [4, 2, 32, 80, 2, 128], P('section', None, 'coil', 'cuts')
Inputs may be any that keep to these rules, and one draw needn't show every extreme that they name: `mask`: 1 marks a sampled phase-encoding line of the slab, 0 one that was not measured.
All inputs are finite; a program needn't handle non-finite values.
Results may differ from a plain program's by a relative error of at most 0.028.
Values may be sent and summed in bfloat16 or wider, within the bound.
A program may use at most 128 MiB of HBM per device.

v0:
```python
import math

import jax
import jax.numpy as jnp
from jax import lax
from jax.sharding import PartitionSpec as P


def extended_2(x, sides, width):
    for axis, dim in sides:
        size, length = (lax.axis_size(axis), x.shape[dim])
        up = [(i, (i + 1) % size) for i in range(size - 1)]
        down = [(j, i) for i, j in up]
        last = lax.slice_in_dim(x, length - width, length, axis=dim)
        leading = lax.slice_in_dim(x, 0, width, axis=dim)
        before = lax.ppermute(last, axis, up)
        after = lax.ppermute(leading, axis, down)
        x = jnp.concatenate([before, x, after], axis=dim)
    return x


def from_everyone(x, axis):
    length = lax.axis_size(axis)
    return lax.all_to_all(jnp.broadcast_to(x[None], (length, *x.shape)), axis, 0, 0, tiled=True)


def laid_out(parts, dim):
    parts = jnp.moveaxis(parts, 0, dim)
    dims = parts.shape
    return parts.reshape(*dims[:dim], dims[dim] * dims[dim + 1], *dims[dim + 2 :])


def collect(x, axis, dim):
    parts = from_everyone(x, axis)
    return laid_out(parts, dim)


def in_blocks(x, dim, length):
    dims = x.shape
    parts = x.reshape(*dims[:dim], length, dims[dim] // length, *dims[dim + 1 :])
    return jnp.moveaxis(parts, dim, 0)


def sum_at_owner(x, axis, dim):
    parts = in_blocks(x, dim, lax.axis_size(axis))
    arrived = lax.all_to_all(parts, axis, split_axis=0, concat_axis=0, tiled=True)
    return arrived.astype(jnp.float32).sum(axis=0)


def passed_along(block, axis, distance):
    devices = range(lax.axis_size(axis))
    route = [(i - distance, i) for i in devices if i - distance in devices]
    return lax.ppermute(block, axis, route)


def dft_table(length, sign):
    ramp = jnp.arange(length, dtype=jnp.int32)
    phase = ramp[:, None] * ramp[None, :] % length
    angle = phase.astype(jnp.float32) * (2.0 * math.pi / length)
    scale = 1.0 / math.sqrt(length)
    cosine = jnp.cos(angle) * scale
    sine = jnp.sin(angle) * (scale * sign)
    upper = jnp.concatenate([cosine, -sine], axis=1)
    lower = jnp.concatenate([sine, cosine], axis=1)
    return jnp.concatenate([upper, lower], axis=0).astype(jnp.bfloat16)


def pass_last(volume, table):
    shape = volume.shape
    flat = volume.reshape(-1, shape[-2] * shape[-1])
    return (
        jnp.dot(flat, table, preferred_element_type=jnp.float32).astype(jnp.bfloat16).reshape(shape)
    )


def pass_middle(volume, table):
    length = volume.shape[1]
    split = table.reshape(2, length, 2, length)
    return jnp.einsum("pjcz,cjdk->pkdz", volume, split, preferred_element_type=jnp.float32).astype(
        jnp.bfloat16
    )


def pass_first(volume, table):
    length = volume.shape[0]
    split = table.reshape(2, length, 2, length)
    return jnp.einsum("jycz,cjdk->kydz", volume, split, preferred_element_type=jnp.float32).astype(
        jnp.bfloat16
    )


def complex_product(sens, image):
    sens_real = sens[:, :, 0].astype(jnp.float32)
    sens_imag = sens[:, :, 1].astype(jnp.float32)
    image_real = image[:, :, 0].astype(jnp.float32)
    image_imag = image[:, :, 1].astype(jnp.float32)
    return jnp.stack(
        [
            sens_real * image_real - sens_imag * image_imag,
            sens_real * image_imag + sens_imag * image_real,
        ],
        axis=2,
    )


def conj_product(sens, back):
    sens_real = sens[:, :, 0].astype(jnp.float32)
    sens_imag = sens[:, :, 1].astype(jnp.float32)
    back_real = back[:, :, 0].astype(jnp.float32)
    back_imag = back[:, :, 1].astype(jnp.float32)
    return jnp.stack(
        [
            sens_real * back_real + sens_imag * back_imag,
            sens_real * back_imag - sens_imag * back_real,
        ],
        axis=2,
    )


def hidden_layer(extended, out_rows, weights_in, bias):
    width = extended.shape[3]
    padded = jnp.pad(extended, ((0, 0), (0, 0), (0, 0), (1, 1)))
    taps = jnp.stack(
        [
            padded[:, shift_row : shift_row + out_rows, :, shift_col : shift_col + width]
            for shift_row in range(3)
            for shift_col in range(3)
        ],
        axis=2,
    )
    taps = taps.reshape(extended.shape[0], out_rows, 18, width)
    summed = jnp.einsum("hf,xyfz->xyhz", weights_in, taps, preferred_element_type=jnp.float32)
    return jax.nn.silu(summed + bias[None, None, :, None]).astype(jnp.bfloat16)


def combine_taps(beside_all, rows):
    width = beside_all.shape[3]
    padded = jnp.pad(beside_all, ((0, 0), (0, 0), (0, 0), (1, 1)))
    total = jnp.zeros((beside_all.shape[0], rows, 2, width), jnp.float32)
    for shift_row in range(3):
        for shift_col in range(3):
            first = (3 * shift_row + shift_col) * 2
            total = (
                total
                + padded[
                    :,
                    shift_row : shift_row + rows,
                    first : first + 2,
                    shift_col : shift_col + width,
                ]
            )
    return total


def refine_rows(current, weights_in, bias, weights_out):
    rows = current.shape[1]
    extended = extended_2(current, (("cuts", 1),), 2)
    hidden = hidden_layer(extended, rows + 2, weights_in, bias)
    first_row = lax.axis_index("cuts") * rows - 1
    global_rows = first_row + jnp.arange(rows + 2, dtype=jnp.int32)
    inside = (global_rows >= 0) & (global_rows < rows * lax.axis_size("cuts"))
    hidden = jnp.where(inside[None, :, None, None], hidden, jnp.zeros((), jnp.bfloat16))
    beside_all = jnp.einsum(
        "fh,xyhz->xyfz", weights_out, hidden, preferred_element_type=jnp.float32
    )
    return combine_taps(beside_all, rows)


def whole_rows(current):
    return collect(current, "cuts", 1)


def sum_gradient(back_rows, size_x):
    full = back_rows(0, size_x)
    folded = sum_at_owner(full.astype(jnp.bfloat16), "cuts", 1)
    grad = sum_at_owner(folded.astype(jnp.bfloat16), "coil", 0)
    return grad


def finish_step(current, grad, step, weights_in, bias, weights_out):
    refine = refine_rows(current, weights_in, bias, weights_out)
    return (current.astype(jnp.float32) - step * grad + refine).astype(jnp.bfloat16)


def cascade_block(current, sens_one, data_one, mask_one, step, weights_in, bias, weights_out):
    halves = whole_rows(current)
    size_y = halves.shape[1]
    size_z = halves.shape[3]
    size_x = halves.shape[0] * lax.axis_size("coil")
    forward_x, forward_y, forward_z = (
        dft_table(size_x, 1.0),
        dft_table(size_y, 1.0),
        dft_table(size_z, 1.0),
    )
    back_x, back_y, back_z = (
        dft_table(size_x, -1.0),
        dft_table(size_y, -1.0),
        dft_table(size_z, -1.0),
    )
    coil_image = complex_product(sens_one, collect(halves, "coil", 0)).astype(jnp.bfloat16)
    partial_value = pass_middle(pass_last(coil_image, forward_z), forward_y)
    predicted = pass_first(partial_value, forward_x)
    weight_mask = mask_one.astype(jnp.float32)[None, :, None, :]
    resid = (weight_mask * (data_one.astype(jnp.float32) - predicted.astype(jnp.float32))).astype(
        jnp.bfloat16
    )
    spectrum = pass_first(resid, back_x)

    def back_rows(start, count):
        back = pass_last(pass_middle(spectrum, back_y), back_z)
        return conj_product(sens_one, back)

    grad = sum_gradient(back_rows, size_x)
    return finish_step(current, grad, step, weights_in, bias, weights_out)


def body(initial, sens, kspace, mask, step_sizes, conv_in, bias_in, conv_out):
    section_count = lax.axis_size("section")
    position = lax.axis_index("section")
    slab_count = initial.shape[0]
    carried = jnp.zeros_like(initial[0])
    results = jnp.zeros((1,) + initial.shape, jnp.bfloat16)
    moments = slab_count + section_count - 1
    for moment in range(moments):
        slab = moment - position
        valid = (slab >= 0) & (slab < slab_count)
        chosen = jnp.clip(slab, 0, slab_count - 1)
        if moment < slab_count:
            fresh = initial[moment]
        else:
            fresh = jnp.zeros_like(initial[0])
        current = jnp.where(position == 0, fresh, carried)
        sens_one = lax.dynamic_index_in_dim(sens, chosen, 0, keepdims=False)[0]
        data_one = lax.dynamic_index_in_dim(kspace, chosen, 0, keepdims=False)[0]
        mask_one = lax.dynamic_index_in_dim(mask, chosen, 0, keepdims=False)
        updated = cascade_block(
            current,
            sens_one,
            data_one,
            mask_one,
            step_sizes[0],
            conv_in[0],
            bias_in[0],
            conv_out[0],
        )
        zero_index = jnp.zeros((), jnp.int32)
        placed = lax.dynamic_update_slice(
            results,
            updated[None, None],
            (zero_index, chosen, zero_index, zero_index, zero_index, zero_index),
        )
        results = jnp.where(valid, placed, results)
        if moment + 1 < moments:
            carried = passed_along(updated, "section", 1)
    return results


def solution(mesh):
    return jax.shard_map(
        body,
        mesh=mesh,
        in_specs=(
            P(None, "coil", "cuts", None, None),
            P(None, ("coil", "cuts"), None, None, None, None),
            P(None, ("coil", "cuts"), None, None, None, None),
            P(),
            P("section"),
            P("section", None, None),
            P("section", None),
            P("section", None, None),
        ),
        out_specs=P("section", None, "coil", "cuts", None, None),
        check_vma=False,
    )
```

profile of v0, /device:TPU:6, one launch (start us, length us, event | category | flops | bytes accessed | tf_op | source)
XLA Modules:
  0.0 525.4 jit_solution(15396388686139940087)
XLA Ops:
  0.8 3.8 all_to_all.100
  5.8 11.9 %all-to-all-start.1 = ((bf16[32,1,80,2,128]{4,2,3,1,0:T(8,128)(2,1)}), bf16[32,1,80,2,128]{4,2,3,1,0:T(8,128)(2,1)}, u32[]{:S(2)}, u32[]{:S(2)}) async-start(bf16[32,1,80,2,128]{4,2,3,1,0:T(8,128)(2,1)} %broadcast_in_dim.82), calls=%async_computation.1 | async-start | bytes 2621440 | tf_op jit(solution)/shard_map/all_to_all | solution.py:24
  17.7 1.8 collective-permute-start
  22.8 15.0 %constant_dynamic-slice_fusion = (bf16[1,1,32,80,2,128]{5,4,3,2,1,0:T(2,128)(2,1)}, bf16[1,1,32,80,2,128]{5,4,3,2,1,0:T(2,128)(2,1)}, bf16[1,1,32,80,2,128]{5,4,...) fusion(bf16[2,1,32,80,2,128]{5,4,3,2,1,0:T(2,128)(2,1)S(1)} %co, ...), kind=kLoop, calls=%fused_computation.544 | loop fusion | bytes 26214420 | tf_op jit(solution)/shard_map/jit(dynamic_index_in_dim)/dynamic_slice | solution.py:234
  39.7 12.3 %all-to-all-done.1 = bf16[32,1,80,2,128]{4,2,3,1,0:T(8,128)(2,1)} async-done(((bf16[32,1,80,2,128]{4,2,3,1,0:T(8,128)(2,1)}), bf16[32,1,80,2,128]{4,2,3,1,0:T(8,128)(2,1)}, u32[]{:S(2)}, u32[]{:S(2)}) %all-to-all-start.1) | async-done | bytes 1310752 | tf_op jit(solution)/shard_map/all_to_all | solution.py:24
  55.4 1.6 convolution_convert_fusion.9
  57.0 2.9 reshape.379
  64.9 1.6 convolution_convert_fusion.8
  66.5 3.3 reshape.381
  69.9 1.8 fusion.326
  72.5 4.8 all_to_all.101
  79.4 5.5 %all-to-all-start.3 = ((bf16[32,1,40,2,128]{4,3,2,1,0:T(2,128)(2,1)}), bf16[32,1,40,2,128]{4,3,2,1,0:T(2,128)(2,1)S(1)}, u32[]{:S(2)}, u32[]{:S(2)}) async-start(bf16[32,1,40,2,128]{4,3,2,1,0:T(2,128)(2,1)} %copy.354), calls=%async_computation.3 | async-start | bytes 1310720 | tf_op jit(solution)/shard_map/all_to_all | solution.py:46
  86.8 18.1 %all-to-all-done.3 = bf16[32,1,40,2,128]{4,3,2,1,0:T(2,128)(2,1)S(1)} async-done(((bf16[32,1,40,2,128]{4,3,2,1,0:T(2,128)(2,1)}), bf16[32,1,40,2,128]{4,3,2,1,0:T(2,128)(2,1)S(1)}, u32[]{:S(2)}, u32[]{:S(2)}) %all-to-all-start.3) | async-done | bytes 655392 | tf_op jit(solution)/shard_map/all_to_all | solution.py:46
  107.1 4.4 collective-permute-done.2
  111.6 3.8 all_to_all.102
  116.6 5.8 %all-to-all-start.5 = ((bf16[32,1,80,2,128]{4,2,3,1,0:T(8,128)(2,1)}), bf16[32,1,80,2,128]{4,2,3,1,0:T(8,128)(2,1)}, u32[]{:S(2)}, u32[]{:S(2)}) async-start(bf16[32,1,80,2,128]{4,2,3,1,0:T(8,128)(2,1)} %broadcast_in_dim.88), calls=%async_computation.5 | async-start | bytes 2621440 | tf_op jit(solution)/shard_map/all_to_all | solution.py:24
  122.5 1.8 collective-permute-start.3
  127.6 29.2 %all-to-all-done.5 = bf16[32,1,80,2,128]{4,2,3,1,0:T(8,128)(2,1)} async-done(((bf16[32,1,80,2,128]{4,2,3,1,0:T(8,128)(2,1)}), bf16[32,1,80,2,128]{4,2,3,1,0:T(8,128)(2,1)}, u32[]{:S(2)}, u32[]{:S(2)}) %all-to-all-start.5) | async-done | bytes 1310752 | tf_op jit(solution)/shard_map/all_to_all | solution.py:24
  161.7 3.1 reshape.386
  169.8 1.6 convolution_convert_fusion.6
  171.5 2.9 reshape.388
  174.4 1.8 fusion.325
  177.0 4.8 all_to_all.103
  182.4 1.6 copy.377
  184.0 5.4 %all-to-all-start.7 = ((bf16[32,1,40,2,128]{4,3,2,1,0:T(2,128)(2,1)}), bf16[32,1,40,2,128]{4,3,2,1,0:T(2,128)(2,1)S(1)}, u32[]{:S(2)}, u32[]{:S(2)}) async-start(bf16[32,1,40,2,128]{4,3,2,1,0:T(2,128)(2,1)} %copy.377), calls=%async_computation.7 | async-start | bytes 1310720 | tf_op jit(solution)/shard_map/all_to_all | solution.py:46
  191.3 18.1 %all-to-all-done.7 = bf16[32,1,40,2,128]{4,3,2,1,0:T(2,128)(2,1)S(1)} async-done(((bf16[32,1,40,2,128]{4,3,2,1,0:T(2,128)(2,1)}), bf16[32,1,40,2,128]{4,3,2,1,0:T(2,128)(2,1)S(1)}, u32[]{:S(2)}, u32[]{:S(2)}) %all-to-all-start.7) | async-done | bytes 655392 | tf_op jit(solution)/shard_map/all_to_all | solution.py:46
  211.6 4.4 collective-permute-done.5
  216.0 3.8 all_to_all.104
  221.0 5.8 %all-to-all-start.9 = ((bf16[32,1,80,2,128]{4,2,3,1,0:T(8,128)(2,1)}), bf16[32,1,80,2,128]{4,2,3,1,0:T(8,128)(2,1)}, u32[]{:S(2)}, u32[]{:S(2)}) async-start(bf16[32,1,80,2,128]{4,2,3,1,0:T(8,128)(2,1)} %broadcast_in_dim.93), calls=%async_computation.9 | async-start | bytes 2621440 | tf_op jit(solution)/shard_map/all_to_all | solution.py:24
  226.9 1.8 collective-permute-start.6
  232.0 29.1 %all-to-all-done.9 = bf16[32,1,80,2,128]{4,2,3,1,0:T(8,128)(2,1)} async-done(((bf16[32,1,80,2,128]{4,2,3,1,0:T(8,128)(2,1)}), bf16[32,1,80,2,128]{4,2,3,1,0:T(8,128)(2,1)}, u32[]{:S(2)}, u32[]{:S(2)}) %all-to-all-start.9) | async-done | bytes 1310752 | tf_op jit(solution)/shard_map/all_to_all | solution.py:24
  264.5 1.7 convolution_convert_fusion.5
  266.2 3.1 reshape.393
  274.3 1.6 convolution_convert_fusion.4
  275.9 2.9 reshape.395
  278.9 1.8 fusion.324
  281.5 4.8 all_to_all.105
  288.4 5.8 %all-to-all-start.11 = ((bf16[32,1,40,2,128]{4,3,2,1,0:T(2,128)(2,1)}), bf16[32,1,40,2,128]{4,3,2,1,0:T(2,128)(2,1)S(1)}, u32[]{:S(2)}, u32[]{:S(2)}) async-start(bf16[32,1,40,2,128]{4,3,2,1,0:T(2,128)(2,1)} %copy.400), calls=%async_computation.11 | async-start | bytes 1310720 | tf_op jit(solution)/shard_map/all_to_all | solution.py:46
  296.1 18.1 %all-to-all-done.11 = bf16[32,1,40,2,128]{4,3,2,1,0:T(2,128)(2,1)S(1)} async-done(((bf16[32,1,40,2,128]{4,3,2,1,0:T(2,128)(2,1)}), bf16[32,1,40,2,128]{4,3,2,1,0:T(2,128)(2,1)S(1)}, u32[]{:S(2)}, u32[]{:S(2)}) %all-to-all-start.11) | async-done | bytes 655392 | tf_op jit(solution)/shard_map/all_to_all | solution.py:46
  316.4 4.4 collective-permute-done.8
  320.8 3.8 all_to_all.106
  325.9 5.8 %all-to-all-start.13 = ((bf16[32,1,80,2,128]{4,2,3,1,0:T(8,128)(2,1)}), bf16[32,1,80,2,128]{4,2,3,1,0:T(8,128)(2,1)}, u32[]{:S(2)}, u32[]{:S(2)}) async-start(bf16[32,1,80,2,128]{4,2,3,1,0:T(8,128)(2,1)} %broadcast_in_dim.98), calls=%async_computation.13 | async-start | bytes 2621440 | tf_op jit(solution)/shard_map/all_to_all | solution.py:24
  333.0 3.0 collective-permute-start.9
  337.1 28.8 %all-to-all-done.13 = bf16[32,1,80,2,128]{4,2,3,1,0:T(8,128)(2,1)} async-done(((bf16[32,1,80,2,128]{4,2,3,1,0:T(8,128)(2,1)}), bf16[32,1,80,2,128]{4,2,3,1,0:T(8,128)(2,1)}, u32[]{:S(2)}, u32[]{:S(2)}) %all-to-all-start.13) | async-done | bytes 1310752 | tf_op jit(solution)/shard_map/all_to_all | solution.py:24
  369.4 1.6 convolution_convert_fusion.3
  371.0 3.1 reshape.400
  380.7 2.9 reshape.402
  383.6 1.8 fusion.323
  386.2 4.8 all_to_all.107
  393.2 5.6 %all-to-all-start.15 = ((bf16[32,1,40,2,128]{4,3,2,1,0:T(2,128)(2,1)}), bf16[32,1,40,2,128]{4,3,2,1,0:T(2,128)(2,1)S(1)}, u32[]{:S(2)}, u32[]{:S(2)}) async-start(bf16[32,1,40,2,128]{4,3,2,1,0:T(2,128)(2,1)} %copy.423), calls=%async_computation.15 | async-start | bytes 1310720 | tf_op jit(solution)/shard_map/all_to_all | solution.py:46
  400.7 18.1 %all-to-all-done.15 = bf16[32,1,40,2,128]{4,3,2,1,0:T(2,128)(2,1)S(1)} async-done(((bf16[32,1,40,2,128]{4,3,2,1,0:T(2,128)(2,1)}), bf16[32,1,40,2,128]{4,3,2,1,0:T(2,128)(2,1)S(1)}, u32[]{:S(2)}, u32[]{:S(2)}) %all-to-all-start.15) | async-done | bytes 655392 | tf_op jit(solution)/shard_map/all_to_all | solution.py:46
  421.0 4.4 collective-permute-done.11
  425.4 3.8 all_to_all.108
  430.4 5.8 %all-to-all-start.17 = ((bf16[32,1,80,2,128]{4,2,3,1,0:T(8,128)(2,1)}), bf16[32,1,80,2,128]{4,2,3,1,0:T(8,128)(2,1)}, u32[]{:S(2)}, u32[]{:S(2)}) async-start(bf16[32,1,80,2,128]{4,2,3,1,0:T(8,128)(2,1)} %broadcast_in_dim.103), calls=%async_computation.17 | async-start | bytes 2621440 | tf_op jit(solution)/shard_map/all_to_all | solution.py:24
  436.3 1.8 collective-permute-start.12
  441.4 29.1 %all-to-all-done.17 = bf16[32,1,80,2,128]{4,2,3,1,0:T(8,128)(2,1)} async-done(((bf16[32,1,80,2,128]{4,2,3,1,0:T(8,128)(2,1)}), bf16[32,1,80,2,128]{4,2,3,1,0:T(8,128)(2,1)}, u32[]{:S(2)}, u32[]{:S(2)}) %all-to-all-start.17) | async-done | bytes 1310752 | tf_op jit(solution)/shard_map/all_to_all | solution.py:24
  475.5 2.9 reshape.407
  483.5 1.6 convolution_convert_fusion
  485.1 2.9 reshape.409
  488.0 1.8 fusion.322
  490.6 4.8 all_to_all.109
  497.6 5.3 %all-to-all-start.19 = ((bf16[32,1,40,2,128]{4,3,2,1,0:T(2,128)(2,1)}), bf16[32,1,40,2,128]{4,3,2,1,0:T(2,128)(2,1)S(1)}, u32[]{:S(2)}, u32[]{:S(2)}) async-start(bf16[32,1,40,2,128]{4,3,2,1,0:T(2,128)(2,1)} %copy.446), calls=%async_computation.19 | async-start | bytes 1310720 | tf_op jit(solution)/shard_map/all_to_all | solution.py:46
  504.8 18.1 %all-to-all-done.19 = bf16[32,1,40,2,128]{4,3,2,1,0:T(2,128)(2,1)S(1)} async-done(((bf16[32,1,40,2,128]{4,3,2,1,0:T(2,128)(2,1)}), bf16[32,1,40,2,128]{4,3,2,1,0:T(2,128)(2,1)S(1)}, u32[]{:S(2)}, u32[]{:S(2)}) %all-to-all-start.19) | async-done | bytes 655392 | tf_op jit(solution)/shard_map/all_to_all | solution.py:46
  523.5 1.7 fusion.271
  (252 shorter events, 101.8 us)
Async XLA Ops:
  0.0 85.4 %copy-start = (bf16[1,18,128]{2,1,0:T(8,128)(2,1)S(1)}, bf16[1,18,128]{2,1,0:T(8,128)(2,1)}, u32[]{:S(2)}) copy-start(bf16[1,18,128]{2,1,0:T(8,128)(2,1)} %param.15) | copy-start | bytes 13828
  5.8 16.9 %copy-start.11 = (s32[2,80,128]{2,1,0:T(8,128)S(1)}, s32[2,80,128]{2,1,0:T(8,128)}, u32[]{:S(2)}) copy-start(s32[2,80,128]{2,1,0:T(8,128)} %param.11) | copy-start | bytes 245764
  5.8 16.9 %copy-start.1 = (bf16[2,1,32,80,2,128]{5,4,3,2,1,0:T(2,128)(2,1)S(1)}, bf16[2,1,32,80,2,128]{5,4,3,2,1,0:T(2,128)(2,1)}, u32[]{:S(2)}) copy-start(bf16[2,1,32,80,2,128]{5,4,3,2,1,0:T(2,128)(2,1)} %param.10) | copy-start | bytes 7864324
  5.8 46.2 %all-to-all-start.1 = ((bf16[32,1,80,2,128]{4,2,3,1,0:T(8,128)(2,1)}), bf16[32,1,80,2,128]{4,2,3,1,0:T(8,128)(2,1)}, u32[]{:S(2)}, u32[]{:S(2)}) async-start(bf16[32,1,80,2,128]{4,2,3,1,0:T(8,128)(2,1)} %broadcast_in_dim.82), calls=%async_computation.1 | async-start | bytes 2621440 | tf_op jit(solution)/shard_map/all_to_all | solution.py:24
  17.7 21.7 %collective-permute-start = (bf16[1,2,2,128]{3,2,1,0:T(2,128)(2,1)S(1)}, bf16[1,2,2,128]{3,2,1,0:T(2,128)(2,1)S(1)}, u32[]{:S(2)}, u32[]{:S(2)}) collective-permute-start(bf16[1,2,2,128]{3,2,1,0:T(2,128)(2,1)S(1)} %get-tuple-element.70), channel_id=1, source_target_pairs={{0,1},{2,3},{4,5},{6,7},{8,9},{10,11},{12,13},{14,15},{16,17},{18,... | collective-permute-start | bytes 3080 | tf_op jit(solution)/shard_map/ppermute | solution.py:16
  19.5 19.9 %collective-permute-start.1 = (bf16[1,2,2,128]{3,2,1,0:T(2,128)(2,1)S(1)}, bf16[1,2,2,128]{3,2,1,0:T(2,128)(2,1)S(1)}, u32[]{:S(2)}, u32[]{:S(2)}) collective-permute-start(bf16[1,2,2,128]{3,2,1,0:T(2,128)(2,1)S(1)} %get-tuple-element.71), channel_id=1, source_target_pairs={{1,0},{3,2},{5,4},{7,6},{9,8},{11,10},{13,12},{15,14},{17,16},{19,... | collective-permute-start | bytes 3080 | tf_op jit(solution)/shard_map/ppermute | solution.py:17
  60.0 1.3 copy-start.10
  79.4 6.0 %copy-start.14 = (bf16[1,128,18]{1,2,0:T(8,128)(2,1)S(1)}, bf16[1,128,18]{1,2,0:T(8,128)(2,1)}, u32[]{:S(2)}) copy-start(bf16[1,128,18]{1,2,0:T(8,128)(2,1)} %param.13) | copy-start | bytes 13828
  79.4 6.1 %copy-start.15 = (f32[1,128]{1,0:T(1,128)S(1)}, f32[1,128]{1,0:T(1,128)}, u32[]{:S(2)}) copy-start(f32[1,128]{1,0:T(1,128)} %param.14) | copy-start | bytes 1540
  79.4 25.5 %all-to-all-start.3 = ((bf16[32,1,40,2,128]{4,3,2,1,0:T(2,128)(2,1)}), bf16[32,1,40,2,128]{4,3,2,1,0:T(2,128)(2,1)S(1)}, u32[]{:S(2)}, u32[]{:S(2)}) async-start(bf16[32,1,40,2,128]{4,3,2,1,0:T(2,128)(2,1)} %copy.354), calls=%async_computation.3 | async-start | bytes 1310720 | tf_op jit(solution)/shard_map/all_to_all | solution.py:46
  86.8 24.7 %copy-start.13 = (bf16[2,1,40,2,128]{4,3,2,1,0:T(2,128)(2,1)S(1)}, bf16[2,1,40,2,128]{4,3,2,1,0:T(2,128)(2,1)}, u32[]{:S(2)}) copy-start(bf16[2,1,40,2,128]{4,3,2,1,0:T(2,128)(2,1)} %param.8) | copy-start | bytes 122884
  105.8 5.7 %collective-permute-start.2 = (bf16[1,40,2,128]{3,2,1,0:T(2,128)(2,1)S(1)}, bf16[1,40,2,128]{3,2,1,0:T(2,128)(2,1)S(1)}, u32[]{:S(2)}, u32[]{:S(2)}) collective-permute-start(bf16[1,40,2,128]{3,2,1,0:T(2,128)(2,1)S(1)} %get-tuple-element.12), channel_id=1, source_target_pairs={{0,64},{64,128},{128,192},{1,65},{65,129},{129,193},{2,66},{66,130... | collective-permute-start | bytes 61448 | tf_op jit(solution)/shard_map/ppermute | solution.py:53
  116.6 8.9 %copy-start.5 = (bf16[1,1,32,80,2,128]{5,4,3,2,1,0:T(2,128)(2,1)S(1)}, bf16[1,1,32,80,2,128]{5,4,3,2,1,0:T(2,128)(2,1)}, u32[]{:S(2)}) copy-start(bf16[1,1,32,80,2,128]{5,4,3,2,1,0:T(2,128)(2,1)} %get-tuple-element.84) | copy-start | bytes 3932164
  116.6 40.1 %all-to-all-start.5 = ((bf16[32,1,80,2,128]{4,2,3,1,0:T(8,128)(2,1)}), bf16[32,1,80,2,128]{4,2,3,1,0:T(8,128)(2,1)}, u32[]{:S(2)}, u32[]{:S(2)}) async-start(bf16[32,1,80,2,128]{4,2,3,1,0:T(8,128)(2,1)} %broadcast_in_dim.88), calls=%async_computation.5 | async-start | bytes 2621440 | tf_op jit(solution)/shard_map/all_to_all | solution.py:24
  122.5 3.3 collective-permute-start.3
  124.3 3.0 collective-permute-start.4
  164.8 1.3 copy-start.9
  184.0 25.4 %all-to-all-start.7 = ((bf16[32,1,40,2,128]{4,3,2,1,0:T(2,128)(2,1)}), bf16[32,1,40,2,128]{4,3,2,1,0:T(2,128)(2,1)S(1)}, u32[]{:S(2)}, u32[]{:S(2)}) async-start(bf16[32,1,40,2,128]{4,3,2,1,0:T(2,128)(2,1)} %copy.377), calls=%async_computation.7 | async-start | bytes 1310720 | tf_op jit(solution)/shard_map/all_to_all | solution.py:46
  210.3 5.7 %collective-permute-start.5 = (bf16[1,40,2,128]{3,2,1,0:T(2,128)(2,1)S(1)}, bf16[1,40,2,128]{3,2,1,0:T(2,128)(2,1)S(1)}, u32[]{:S(2)}, u32[]{:S(2)}) collective-permute-start(bf16[1,40,2,128]{3,2,1,0:T(2,128)(2,1)S(1)} %get-tuple-element.10), channel_id=1, source_target_pairs={{0,64},{64,128},{128,192},{1,65},{65,129},{129,193},{2,66},{66,130... | collective-permute-start | bytes 61448 | tf_op jit(solution)/shard_map/ppermute | solution.py:53
  221.0 9.0 %copy-start.4 = (bf16[1,1,32,80,2,128]{5,4,3,2,1,0:T(2,128)(2,1)S(1)}, bf16[1,1,32,80,2,128]{5,4,3,2,1,0:T(2,128)(2,1)}, u32[]{:S(2)}) copy-start(bf16[1,1,32,80,2,128]{5,4,3,2,1,0:T(2,128)(2,1)} %get-tuple-element.85) | copy-start | bytes 3932164
  221.0 40.1 %all-to-all-start.9 = ((bf16[32,1,80,2,128]{4,2,3,1,0:T(8,128)(2,1)}), bf16[32,1,80,2,128]{4,2,3,1,0:T(8,128)(2,1)}, u32[]{:S(2)}, u32[]{:S(2)}) async-start(bf16[32,1,80,2,128]{4,2,3,1,0:T(8,128)(2,1)} %broadcast_in_dim.93), calls=%async_computation.9 | async-start | bytes 2621440 | tf_op jit(solution)/shard_map/all_to_all | solution.py:24
  226.9 3.3 collective-permute-start.6
  228.7 3.0 collective-permute-start.7
  269.3 1.3 copy-start.8
  288.4 25.8 %all-to-all-start.11 = ((bf16[32,1,40,2,128]{4,3,2,1,0:T(2,128)(2,1)}), bf16[32,1,40,2,128]{4,3,2,1,0:T(2,128)(2,1)S(1)}, u32[]{:S(2)}, u32[]{:S(2)}) async-start(bf16[32,1,40,2,128]{4,3,2,1,0:T(2,128)(2,1)} %copy.400), calls=%async_computation.11 | async-start | bytes 1310720 | tf_op jit(solution)/shard_map/all_to_all | solution.py:46
  315.1 5.7 %collective-permute-start.8 = (bf16[1,40,2,128]{3,2,1,0:T(2,128)(2,1)S(1)}, bf16[1,40,2,128]{3,2,1,0:T(2,128)(2,1)S(1)}, u32[]{:S(2)}, u32[]{:S(2)}) collective-permute-start(bf16[1,40,2,128]{3,2,1,0:T(2,128)(2,1)S(1)} %get-tuple-element.8), channel_id=1, source_target_pairs={{0,64},{64,128},{128,192},{1,65},{65,129},{129,193},{2,66},{66,130... | collective-permute-start | bytes 61448 | tf_op jit(solution)/shard_map/ppermute | solution.py:53
  325.9 10.2 %copy-start.3 = (bf16[1,1,32,80,2,128]{5,4,3,2,1,0:T(2,128)(2,1)S(1)}, bf16[1,1,32,80,2,128]{5,4,3,2,1,0:T(2,128)(2,1)}, u32[]{:S(2)}) copy-start(bf16[1,1,32,80,2,128]{5,4,3,2,1,0:T(2,128)(2,1)} %get-tuple-element.82) | copy-start | bytes 3932164
  325.9 40.1 %all-to-all-start.13 = ((bf16[32,1,80,2,128]{4,2,3,1,0:T(8,128)(2,1)}), bf16[32,1,80,2,128]{4,2,3,1,0:T(8,128)(2,1)}, u32[]{:S(2)}, u32[]{:S(2)}) async-start(bf16[32,1,80,2,128]{4,2,3,1,0:T(8,128)(2,1)} %broadcast_in_dim.98), calls=%async_computation.13 | async-start | bytes 2621440 | tf_op jit(solution)/shard_map/all_to_all | solution.py:24
  331.7 4.5 collective-permute-start.10
  333.0 3.8 collective-permute-start.9
  374.1 1.3 copy-start.7
  393.2 25.6 %all-to-all-start.15 = ((bf16[32,1,40,2,128]{4,3,2,1,0:T(2,128)(2,1)}), bf16[32,1,40,2,128]{4,3,2,1,0:T(2,128)(2,1)S(1)}, u32[]{:S(2)}, u32[]{:S(2)}) async-start(bf16[32,1,40,2,128]{4,3,2,1,0:T(2,128)(2,1)} %copy.423), calls=%async_computation.15 | async-start | bytes 1310720 | tf_op jit(solution)/shard_map/all_to_all | solution.py:46
  419.7 10.8 %copy-start.12 = (bf16[1,2,1,40,2,128]{5,4,3,2,1,0:T(2,128)(2,1)}, bf16[1,2,1,40,2,128]{5,4,3,2,1,0:T(2,128)(2,1)S(1)}, u32[]{:S(2)}) copy-start(bf16[1,2,1,40,2,128]{5,4,3,2,1,0:T(2,128)(2,1)S(1)} %get-tuple-element.5) | copy-start | bytes 122884
  419.7 5.7 %collective-permute-start.11 = (bf16[1,40,2,128]{3,2,1,0:T(2,128)(2,1)S(1)}, bf16[1,40,2,128]{3,2,1,0:T(2,128)(2,1)S(1)}, u32[]{:S(2)}, u32[]{:S(2)}) collective-permute-start(bf16[1,40,2,128]{3,2,1,0:T(2,128)(2,1)S(1)} %get-tuple-element.6), channel_id=1, source_target_pairs={{0,64},{64,128},{128,192},{1,65},{65,129},{129,193},{2,66},{66,130... | collective-permute-start | bytes 61448 | tf_op jit(solution)/shard_map/ppermute | solution.py:53
  430.4 9.0 %copy-start.2 = (bf16[1,1,32,80,2,128]{5,4,3,2,1,0:T(2,128)(2,1)S(1)}, bf16[1,1,32,80,2,128]{5,4,3,2,1,0:T(2,128)(2,1)}, u32[]{:S(2)}) copy-start(bf16[1,1,32,80,2,128]{5,4,3,2,1,0:T(2,128)(2,1)} %get-tuple-element.86) | copy-start | bytes 3932164
  430.4 40.1 %all-to-all-start.17 = ((bf16[32,1,80,2,128]{4,2,3,1,0:T(8,128)(2,1)}), bf16[32,1,80,2,128]{4,2,3,1,0:T(8,128)(2,1)}, u32[]{:S(2)}, u32[]{:S(2)}) async-start(bf16[32,1,80,2,128]{4,2,3,1,0:T(8,128)(2,1)} %broadcast_in_dim.103), calls=%async_computation.17 | async-start | bytes 2621440 | tf_op jit(solution)/shard_map/all_to_all | solution.py:24
  436.3 3.3 collective-permute-start.12
  438.1 3.0 collective-permute-start.13
  478.5 1.3 copy-start.6
  497.6 25.4 %all-to-all-start.19 = ((bf16[32,1,40,2,128]{4,3,2,1,0:T(2,128)(2,1)}), bf16[32,1,40,2,128]{4,3,2,1,0:T(2,128)(2,1)S(1)}, u32[]{:S(2)}, u32[]{:S(2)}) async-start(bf16[32,1,40,2,128]{4,3,2,1,0:T(2,128)(2,1)} %copy.446), calls=%async_computation.19 | async-start | bytes 1310720 | tf_op jit(solution)/shard_map/all_to_all | solution.py:46
where the time goes:
time: 531 us; the launch traced here: 525 us
  waiting for transfers between devices  242 us (46%)
  local copies, waits for them, and re-layouts  98.6 us (19%)
  starting transfers between devices  84.5 us (16%)
  blocking collectives  42.7 us (8%)
  matrix products  37 us (7%)
  other arithmetic  18.5 us (3%)
    all_to_all x5, waiting for transfers between devices, from_everyone(): lax.all_to_all(jnp.broadcast_to(x[None], (length, *x.shape)), axis, 0, 0,...  129 us
    all_to_all x5, waiting for transfers between devices, sum_at_owner(): lax.all_to_all(parts, axis, split_axis=0, concat_axis=0, tiled=True)  90.6 us
    all_to_all x5, starting transfers between devices, from_everyone(): lax.all_to_all(jnp.broadcast_to(x[None], (length, *x.shape)), axis, 0, 0,...  35.1 us
    reshape x10, local copies, waits for them, and re-layouts, pass_last(): jnp.dot(flat, table, preferred_element_type=jnp.float32)  30.4 us
    all_to_all x5, starting transfers between devices, sum_at_owner(): lax.all_to_all(parts, axis, split_axis=0, concat_axis=0, tiled=True)  27.5 us
    all_to_all x5, blocking collectives, sum_at_owner(): lax.all_to_all(parts, axis, split_axis=0, concat_axis=0, tiled=True)  23.9 us
    all_to_all x5, blocking collectives, from_everyone(): lax.all_to_all(jnp.broadcast_to(x[None], (length, *x.shape)), axis, 0, 0,...  18.8 us
    ppermute x4, waiting for transfers between devices, passed_along(): return lax.ppermute(block, axis, route)  17.5 us
  transfers between devices with their start and end apart: 24, of which 18 were waited for; matrix products, arithmetic and copies ran while one was open for 6% of the time, Pallas kernels for 0%

commit v1 on v0

v1 whole, which is shorter than its diff:
```python
import functools
import math

import jax
import jax.numpy as jnp
import ml_dtypes
import numpy as np
from jax import lax
from jax.experimental import pallas as pl
from jax.experimental.pallas import tpu as pltpu
from jax.sharding import PartitionSpec as P

MESH = pl.DeviceIdType.MESH
BF = jnp.bfloat16
F32 = jnp.float32
SIZE_X, SIZE_Y, SIZE_Z = 32, 80, 128
ROWS = 2 * SIZE_Y
HID = 128
CASCADES = 4
SLOTS = 16


def dft_table(length, sign):
    ramp = np.arange(length)
    angle = (ramp[:, None] * ramp[None, :] % length) * (2.0 * math.pi / length)
    cosine = np.cos(angle) / math.sqrt(length)
    sine = sign * np.sin(angle) / math.sqrt(length)
    return np.block([[cosine, -sine], [sine, cosine]])


def constants():
    planar = np.arange(ROWS)
    woven = 2 * (planar % SIZE_Y) + planar // SIZE_Y
    deal = np.zeros((ROWS, ROWS))
    deal[planar, woven] = 1.0
    forward_y = dft_table(SIZE_Y, 1.0).T
    back_y = dft_table(SIZE_Y, -1.0).T
    square = np.concatenate([back_y @ deal, forward_y, back_y, deal, deal.T], axis=0)
    wide = np.concatenate([dft_table(SIZE_Z, 1.0), dft_table(SIZE_Z, -1.0)], axis=0)
    taps = np.zeros((SIZE_Y * 8, ROWS + 16))
    gather = np.zeros((ROWS, SIZE_Y * 8))
    for row in range(SIZE_Y):
        taps[row * 8 + 6, ROWS] = 1.0
        for shift in range(3):
            other = row + shift - 1
            if 0 <= other < SIZE_Y:
                for part in range(2):
                    taps[row * 8 + shift * 2 + part, part * SIZE_Y + other] = 1.0
                    gather[part * SIZE_Y + row, other * 8 + shift * 2 + part] = 1.0
    place_in = np.zeros((18, 128))
    place_out = np.zeros((32, 18))
    for shift_row in range(3):
        for shift_col in range(3):
            for part in range(2):
                place = shift_col * 8 + shift_row * 2 + part
                column = (3 * shift_row + shift_col) * 2 + part
                place_in[column, place] = 1.0
                place_out[place, column] = 1.0
    return [part.astype(ml_dtypes.bfloat16) for part in (square, wide, taps, gather, place_in, place_out)]


def twiddles():
    first = np.zeros((2, 4, 4), np.complex128)
    second = np.zeros((2, 4, 4, 4), np.complex128)
    for odd in range(2):
        for k in range(4):
            for a in range(4):
                first[odd, k, a] = np.exp(2j * math.pi * k * (2 * a + odd) / 8)
                for b in range(4):
                    position = 8 * b + 2 * a + odd
                    second[odd, k, b, a] = np.exp(2j * math.pi * k * position / SIZE_X) / math.sqrt(SIZE_X)
    return first, second


def dot(a, b):
    return jnp.dot(a, b, preferred_element_type=F32)


def by_lanes(x):
    return jnp.concatenate([x[:SIZE_Y], x[SIZE_Y:]], axis=1)


def by_rows(x):
    return jnp.concatenate([x[:, :SIZE_Z], x[:, SIZE_Z:]], axis=0)


def swap_pair(x):
    a, b, c, d = x[:SIZE_Y, :SIZE_Z], x[SIZE_Y:, :SIZE_Z], x[:SIZE_Y, SIZE_Z:], x[SIZE_Y:, SIZE_Z:]
    return jnp.concatenate(
        [jnp.concatenate([a, b], axis=1), jnp.concatenate([c, d], axis=1)], axis=0
    )


def swap_back(x):
    a, b, c, d = x[:SIZE_Y, :SIZE_Z], x[:SIZE_Y, SIZE_Z:], x[SIZE_Y:, :SIZE_Z], x[SIZE_Y:, SIZE_Z:]
    return jnp.concatenate(
        [jnp.concatenate([a, b], axis=0), jnp.concatenate([c, d], axis=0)], axis=1
    )


def conj_times(s, t):
    s_real, s_imag = s[:, :SIZE_Z].astype(F32), s[:, SIZE_Z:].astype(F32)
    t_real, t_imag = t[:, :SIZE_Z], t[:, SIZE_Z:]
    return s_real * t_real + s_imag * t_imag, s_real * t_imag - s_imag * t_real


def kernel(
    initial, sens, kspace, mask, step, conv_in, bias, conv_out,
    square_in, wide_in, taps_in, gather_in, place_in, place_out,
    out,
    square, wide, taps_sel, gather_sel,
    kbuf, ubuf, gbuf, tbuf, sown, bpart, brecv, bsum, bin_, btot,
    srecv, splan, ibuf, wbuf, fbuf, mplan, mwoven,
    vbuf, wspec, partial, arrived, tapbuf, prodbuf, obuf,
    local_sem, own_sem, s_send, s_recv, i_send, i_recv, w_send, w_recv,
    x_send, x_recv, b_send, b_recv, r_send, r_recv, o_send, o_recv,
):
    sec, pos, core = lax.axis_index("section"), lax.axis_index("coil"), lax.axis_index("cuts")
    row, col = pos // 8, pos % 8
    odd_col = col % 2
    sign = 1 - 2 * odd_col
    odd = sec % 2
    slab = sec // 2
    home = odd_col == odd

    def at(section, y, z, c):
        return (section, y * 8 + z, c)

    twin = col + sign
    mates = [at(sec, row, col, 1 - core), at(sec, row, twin, core), at(sec, row, twin, 1 - core)]
    others = [((sec + k) % 4, pos, core) for k in (1, 2, 3)]

    def toward(j, dy):
        z = (col + (1 - 2 * (j % 2)) * sign * j + 8) % 8
        y = (row + dy) % 4
        return at(sec, y, z, core), 8 * y + 2 * (z // 2) + odd, y * 4 + z // 2

    loads = [
        pltpu.make_async_copy(square_in, square, local_sem.at[0]),
        pltpu.make_async_copy(kspace.at[slab], kbuf, local_sem.at[1]),
        pltpu.make_async_copy(wide_in, wide, local_sem.at[2]),
        pltpu.make_async_copy(taps_in, taps_sel, local_sem.at[3]),
        pltpu.make_async_copy(gather_in, gather_sel, local_sem.at[4]),
    ]
    own_loads = []
    for slot in range(SLOTS):
        _, position, _ = toward(slot // 4, slot % 4)
        own_loads.append(pltpu.make_async_copy(sens.at[slab, position], sown.at[slot], own_sem.at[slot]))
    for load in loads + own_loads:
        load.start()

    barrier = pltpu.get_barrier_semaphore()
    greet = list(mates) + list(others)
    for offset in (0, 2, -1, -3, -2):
        for dy in range(4):
            if offset or dy:
                greet.append(at(sec, (row + dy) % 4, (col + sign * offset + 8) % 8, core))
    for device in greet:
        pl.semaphore_signal(barrier, inc=1, device_id=device, device_id_type=MESH)
    pl.semaphore_wait(barrier, len(greet))

    def remote(src, dst, send, recv, device):
        return pltpu.make_async_remote_copy(
            src_ref=src, dst_ref=dst, send_sem=send, recv_sem=recv, device_id=device, device_id_type=MESH
        )

    half = pl.multiple_of(core * SIZE_Y, SIZE_Y)
    image_copies = [
        remote(initial.at[slab], ibuf.at[pl.ds(half, SIZE_Y)], i_send.at[k], i_recv.at[core], mates[k])
        for k in range(3)
    ]

    @pl.when(home)
    def _():
        for copy in image_copies:
            copy.start()
        ibuf[pl.ds(half, SIZE_Y)] = initial[slab]

    sens_copies = []
    for slot in range(1, SLOTS):
        device, position, _ = toward(slot // 4, slot % 4)
        sens_copies.append(
            remote(sens.at[slab, position], srecv.at[slot], s_send.at[slot], s_recv.at[slot], device)
        )
    for copy in sens_copies:
        copy.start()

    bias_rows = jnp.broadcast_to(bias[...], (128, 128))
    high = bias_rows.astype(BF).astype(F32)
    middle = (bias_rows - high).astype(BF).astype(F32)
    low = bias_rows - high - middle
    which = lax.broadcasted_iota(jnp.int32, (128, 128), 0)
    stacked = jnp.where(which == 6, high, jnp.where(which == 14, middle, jnp.where(which == 22, low, 0.0)))
    first_layer = dot(conv_in[0], place_in[...]) + stacked.T
    wbuf[sec, 0:128] = (0.5 * first_layer).astype(BF)
    wbuf[sec, 128:160] = dot(place_out[...], conv_out[0]).astype(BF)
    fbuf[sec] = jnp.full((8, 128), step[0], F32)
    net_copies = []
    for k in range(3):
        net_copies.append(remote(wbuf.at[sec], wbuf.at[sec], w_send.at[k], w_recv.at[sec], others[k]))
        net_copies.append(remote(fbuf.at[sec], fbuf.at[sec], w_send.at[3 + k], w_recv.at[4 + sec], others[k]))
    for copy in net_copies:
        copy.start()

    loads[0].wait()
    plane = mask[slab].astype(F32).astype(BF)
    both = jnp.concatenate([plane, plane], axis=0)
    mplan[...] = jnp.concatenate([both, both], axis=1)
    mwoven[...] = dot(square[4 * ROWS : 5 * ROWS], both).astype(BF)
    loads[1].wait()

    fold = (1 - 2 * odd).astype(F32)

    def data_rows(n, _):
        masked = mwoven[...]
        two = jnp.concatenate([kbuf[n] * masked, kbuf[n + 16] * masked], axis=1)
        done = dot(square[0:ROWS], two)
        ubuf[n] = done[:, :SIZE_Z] + fold * done[:, SIZE_Z:]
        return 0

    lax.fori_loop(0, 16, data_rows, 0)

    first, second = twiddles()

    def coefficient(table):
        even_value, odd_value = complex(table[0]), complex(table[1])
        return (
            jnp.where(odd == 0, np.float32(even_value.real), np.float32(odd_value.real)),
            jnp.where(odd == 0, np.float32(even_value.imag), np.float32(odd_value.imag)),
        )

    def weighted(terms):
        real, imag = None, None
        for (w_real, w_imag), (v_real, v_imag) in terms:
            r = w_real * v_real - w_imag * v_imag
            i = w_real * v_imag + w_imag * v_real
            real, imag = (r, i) if real is None else (real + r, imag + i)
        return real, imag

    def x_pass(chunk, _):
        top = pl.multiple_of(chunk * 16, 16)
        below = pl.multiple_of(SIZE_Y + chunk * 16, 16)
        for n in range(4):
            u = [(ubuf[n + 4 * k, pl.ds(top, 16)], ubuf[n + 4 * k, pl.ds(below, 16)]) for k in range(4)]
            for a in range(4):
                real, imag = weighted([(coefficient(first[:, k, a]), u[k]) for k in range(4)])
                gbuf[n * 4 + a, 0:16] = real
                gbuf[n * 4 + a, 16:32] = imag
        for a in range(4):
            g = [(gbuf[n * 4 + a, 0:16], gbuf[n * 4 + a, 16:32]) for n in range(4)]
            for b in range(4):
                real, imag = weighted([(coefficient(second[:, n, b, a]), g[n]) for n in range(4)])
                tbuf[b * 4 + a, pl.ds(top, 16), 0:SIZE_Z] = real.astype(BF)
                tbuf[b * 4 + a, pl.ds(top, 16), SIZE_Z:] = imag.astype(BF)
        return 0

    lax.fori_loop(0, 5, x_pass, 0)
    loads[2].wait()
    for load in own_loads:
        load.wait()

    def share(parity):
        def one(q, _):
            jh = q // 2
            j = 2 * jh + parity
            dy = 2 * (q % 2)
            _, _, e0 = toward(j, dy)
            _, _, e1 = toward(j, dy + 1)
            done = dot(jnp.concatenate([tbuf[e0], tbuf[e1]], axis=0), wide[256:512])
            slot = j * 4 + dy
            pair = dot(square[3 * ROWS : 4 * ROWS], jnp.concatenate([sown[slot], sown[slot + 1]], axis=1))
            pair = swap_pair(pair)
            for k in range(2):
                real, imag = conj_times(pair[k * SIZE_Y : (k + 1) * SIZE_Y], done[k * SIZE_Y : (k + 1) * SIZE_Y])
                bpart[parity, jh * 4 + dy + k] = jnp.concatenate([real, imag], axis=1).astype(BF)
            return 0

        lax.fori_loop(0, 4, one, 0)

    share(1 - core)
    exchange = remote(bpart.at[1 - core], brecv, x_send, x_recv, mates[0])
    exchange.start()
    share(core)
    exchange.wait_recv()

    for q in range(8):
        bsum[q] = (bpart[core, q].astype(F32) + brecv[q].astype(F32)).astype(BF)
    data_copies = []
    for q in range(8):
        device, _, _ = toward(2 * (q // 4) + core, q % 4)
        data_copies.append(remote(bsum.at[q], bin_.at[q], b_send.at[q], b_recv.at[q], device))

    @pl.when(core == 0)
    def _():
        bin_[0] = bsum[0]

    @pl.when(core == 1)
    def _():
        data_copies[0].start()

    for copy in data_copies[1:]:
        copy.start()

    def arrival(index):
        return remote(ibuf.at[pl.ds(index * SIZE_Y, SIZE_Y)], ibuf.at[pl.ds(index * SIZE_Y, SIZE_Y)],
                      i_send.at[0], i_recv.at[index], mates[0])

    @pl.when(jnp.logical_or(jnp.logical_not(home), core == 1))
    def _():
        arrival(0).wait_recv()

    @pl.when(jnp.logical_or(jnp.logical_not(home), core == 0))
    def _():
        arrival(1).wait_recv()

    image = by_lanes(dot(square[3 * ROWS : 4 * ROWS], ibuf[...]))

    for k in range(8):
        if k:
            sens_copies[2 * k - 1].wait_recv()
        sens_copies[2 * k].wait_recv()
        left = sown[0] if k == 0 else srecv[2 * k]
        pair = dot(square[3 * ROWS : 4 * ROWS], jnp.concatenate([left, srecv[2 * k + 1]], axis=1))
        splan[pl.ds(k * ROWS, ROWS)] = swap_pair(pair).astype(BF)

    loads[3].wait()
    loads[4].wait()
    lane = lax.broadcasted_iota(jnp.int32, (ROWS, SIZE_Z), 1)

    def moved_right(x):
        return jnp.where(lane == 0, 0.0, pltpu.roll(x, 1, 1))

    def moved_left(x):
        return jnp.where(lane == SIZE_Z - 1, 0.0, pltpu.roll(x, SIZE_Z - 1, 1))

    def net_arrival(c, buf, index):
        return remote(buf.at[c], buf.at[c], w_send.at[0], w_recv.at[index], others[0])

    for k in range(3):
        other = (sec + k + 1) % 4
        net_arrival(other, wbuf, other).wait_recv()
        net_arrival(other, fbuf, 4 + other).wait_recv()

    def operator(image):
        real, imag = image[:, :SIZE_Z], image[:, SIZE_Z:]
        for k in range(SLOTS):
            s = splan[pl.ds(k * SIZE_Y, SIZE_Y)].astype(F32)
            s_real, s_imag = s[:, :SIZE_Z], s[:, SIZE_Z:]
            v = jnp.concatenate([s_real * real - s_imag * imag, s_real * imag + s_imag * real], axis=1)
            vbuf[pl.ds(k * SIZE_Y, SIZE_Y)] = v.astype(BF)
        for k in range(8):
            spectrum = dot(vbuf[pl.ds(k * ROWS, ROWS)], wide[0:256]).astype(BF)
            wspec[pl.ds(k * ROWS, ROWS)] = swap_back(spectrum)
        for k in range(8):
            predicted = dot(square[ROWS : 2 * ROWS], wspec[pl.ds(k * ROWS, ROWS)]).astype(BF)
            vbuf[pl.ds(k * ROWS, ROWS)] = predicted * mplan[...]
        for k in range(8):
            back = dot(square[2 * ROWS : 3 * ROWS], vbuf[pl.ds(k * ROWS, ROWS)]).astype(BF)
            wspec[pl.ds(k * ROWS, ROWS)] = swap_pair(back)
        total_real, total_imag = jnp.zeros((SIZE_Y, SIZE_Z), F32), jnp.zeros((SIZE_Y, SIZE_Z), F32)
        for k in range(8):
            back = dot(wspec[pl.ds(k * ROWS, ROWS)], wide[256:512])
            for i in range(2):
                s = splan[pl.ds(k * ROWS + i * SIZE_Y, SIZE_Y)]
                r, m = conj_times(s, back[i * SIZE_Y : (i + 1) * SIZE_Y])
                total_real, total_imag = total_real + r, total_imag + m
        return jnp.concatenate([total_real, total_imag], axis=1)

    def refine(image, c):
        planar = by_rows(image)
        three = jnp.concatenate([moved_right(planar), planar, moved_left(planar)], axis=1)
        lift = jnp.where(lax.broadcasted_iota(jnp.int32, (16, 3 * SIZE_Z), 0) == 0, 1.0, 0.0)
        operand = jnp.concatenate([three, lift], axis=0).astype(BF)
        tapbuf[...] = dot(taps_sel[...], operand)
        zero = jnp.zeros((8, SIZE_Z), F32)

        def rows_of(step_index, _):
            for i in range(4):
                base = pl.multiple_of(step_index * 64 + i * 16, 16)
                eight = [tapbuf[pl.ds(base + 8 * k, 8)] for k in range(2)]
                columns = [
                    jnp.concatenate([e[:, 0:128], e[:, 128:256], e[:, 256:384], zero], axis=0) for e in eight
                ]
                near = jnp.concatenate(columns, axis=1).astype(BF)
                pre = dot(wbuf[c, 0:128][:, 0:32], near)
                hidden = (pre + pre * jnp.tanh(pre)).astype(BF)
                product = dot(wbuf[c, 128:160], hidden)
                for k in range(2):
                    for d in range(3):
                        prodbuf[pl.ds(base + 8 * k, 8), d * 128 : (d + 1) * 128] = product[
                            d * 8 : (d + 1) * 8, k * 128 : (k + 1) * 128
                        ]
            return 0

        lax.fori_loop(0, 10, rows_of, 0)
        summed = dot(gather_sel[...], prodbuf[...].astype(BF))
        total = moved_right(summed[:, 0:128]) + summed[:, 128:256] + moved_left(summed[:, 256:384])
        return by_lanes(total)

    def data_arrival(q):
        return remote(bsum.at[q], bin_.at[q], b_send.at[q], b_recv.at[q], mates[0])

    def out_copy(c):
        return remote(obuf.at[c], out.at[slab], o_send.at[c], o_recv.at[slab], (c, pos, core))

    def cascade(c, image):
        sent = operator(image)

        @pl.when(c == 0)
        def _():
            @pl.when(core == 1)
            def _():
                data_arrival(0).wait_recv()

            for q in range(1, 8):
                data_arrival(q).wait_recv()
            total = bin_[0].astype(F32)
            for q in range(1, 8):
                total = total + bin_[q].astype(F32)
            btot[...] = total

        partial[c] = (sent - btot[...]).astype(BF)
        copies = [
            remote(partial.at[c], arrived.at[c, k], r_send.at[c, k], r_recv.at[c, k], mates[k]) for k in range(3)
        ]
        for copy in copies:
            copy.start()
        refined = refine(image, c)
        for copy in copies:
            copy.wait_recv()
        total = partial[c].astype(F32)
        for k in range(3):
            total = total + arrived[c, k].astype(F32)
        updated = (image + fbuf[c, 0:1, 0:1] * total + refined).astype(BF)

        @pl.when(home)
        def _():
            base = pl.multiple_of(4 * ROWS + core * SIZE_Y, 16)
            obuf[c] = dot(square[pl.ds(base, SIZE_Y)], by_rows(updated)).astype(BF)

            @pl.when(c == sec)
            def _():
                out[slab] = obuf[c]

            @pl.when(c != sec)
            def _():
                out_copy(c).start()

        return updated.astype(F32)

    lax.fori_loop(0, CASCADES, cascade, image)

    for c in range(CASCADES):
        for k in range(3):
            remote(partial.at[c], arrived.at[c, k], r_send.at[c, k], r_recv.at[c, k], mates[k]).wait_send()

        @pl.when(jnp.logical_and(home, c != sec))
        def _():
            out_copy(c).wait_send()

    for m in range(2):

        @pl.when(2 * m + odd_col != sec)
        def _():
            remote(obuf.at[0], out.at[m], o_send.at[0], o_recv.at[m], others[0]).wait_recv()

    @pl.when(home)
    def _():
        for copy in image_copies:
            copy.wait_send()

    for copy in sens_copies + net_copies + [exchange] + data_copies[1:]:
        copy.wait_send()

    @pl.when(core == 1)
    def _():
        data_copies[0].wait_send()


def body(initial, sens, kspace, mask, step_sizes, conv_in, bias_in, conv_out):
    slabs = initial.shape[0]
    initial = initial.reshape(slabs, SIZE_Y, SIZE_Z)
    sens = sens.reshape(slabs, SIZE_X, ROWS, SIZE_Z)
    kspace = kspace.reshape(slabs, SIZE_X, ROWS, SIZE_Z)
    tables = [jnp.asarray(part) for part in constants()]
    vmem = pl.BlockSpec(memory_space=pltpu.VMEM)
    hbm = pl.BlockSpec(memory_space=pltpu.HBM)
    smem = pl.BlockSpec(memory_space=pltpu.SMEM)
    dma = pltpu.SemaphoreType.DMA
    slice_shape = (SIZE_Y, 2 * SIZE_Z)
    scratch = [
        pltpu.VMEM((5 * ROWS, ROWS), BF),
        pltpu.VMEM((512, 256), BF),
        pltpu.VMEM((SIZE_Y * 8, ROWS + 16), BF),
        pltpu.VMEM((ROWS, SIZE_Y * 8), BF),
        pltpu.VMEM((SIZE_X, ROWS, SIZE_Z), BF),
        pltpu.VMEM((16, ROWS, SIZE_Z), F32),
        pltpu.VMEM((16, 32, SIZE_Z), F32),
        pltpu.VMEM((16, *slice_shape), BF),
        pltpu.VMEM((SLOTS, ROWS, SIZE_Z), BF),
        pltpu.VMEM((2, 8, *slice_shape), BF),
        pltpu.VMEM((8, *slice_shape), BF),
        pltpu.VMEM((8, *slice_shape), BF),
        pltpu.VMEM((8, *slice_shape), BF),
        pltpu.VMEM(slice_shape, F32),
        pltpu.VMEM((SLOTS, ROWS, SIZE_Z), BF),
        pltpu.VMEM((SLOTS * SIZE_Y, 2 * SIZE_Z), BF),
        pltpu.VMEM((ROWS, SIZE_Z), BF),
        pltpu.VMEM((CASCADES, 160, 128), BF),
        pltpu.VMEM((CASCADES, 8, 128), F32),
        pltpu.VMEM((ROWS, 2 * SIZE_Z), BF),
        pltpu.VMEM((ROWS, SIZE_Z), BF),
        pltpu.VMEM((SLOTS * SIZE_Y, 2 * SIZE_Z), BF),
        pltpu.VMEM((SLOTS * SIZE_Y, 2 * SIZE_Z), BF),
        pltpu.VMEM((CASCADES, *slice_shape), BF),
        pltpu.VMEM((CASCADES, 3, *slice_shape), BF),
        pltpu.VMEM((SIZE_Y * 8, 3 * SIZE_Z), F32),
        pltpu.VMEM((SIZE_Y * 8, 3 * SIZE_Z), F32),
        pltpu.VMEM((CASCADES, SIZE_Y, SIZE_Z), BF),
        dma((5,)),
        dma((SLOTS,)),
        dma((SLOTS,)),
        dma((SLOTS,)),
        dma((3,)),
        dma((2,)),
        dma((6,)),
        dma((8,)),
        dma,
        dma,
        dma((8,)),
        dma((8,)),
        dma((CASCADES, 3)),
        dma((CASCADES, 3)),
        dma((CASCADES,)),
        dma((2,)),
    ]
    result = pl.pallas_call(
        kernel,
        out_shape=jax.ShapeDtypeStruct((slabs, SIZE_Y, SIZE_Z), BF),
        in_specs=[vmem, hbm, hbm, vmem, smem, vmem, vmem, vmem, hbm, hbm, hbm, hbm, vmem, vmem],
        out_specs=vmem,
        scratch_shapes=scratch,
        compiler_params=pltpu.CompilerParams(
            collective_id=0, has_side_effects=True, vmem_limit_bytes=40 << 20
        ),
    )(initial, sens, kspace, mask, step_sizes, conv_in, bias_in, conv_out, *tables)
    return result.reshape(1, slabs, 1, SIZE_Y // 2, 2, SIZE_Z)


def solution(mesh):
    return jax.shard_map(
        body,
        mesh=mesh,
        in_specs=(
            P(None, "coil", "cuts", None, None),
            P(None, ("coil", "cuts"), None, None, None, None),
            P(None, ("coil", "cuts"), None, None, None, None),
            P(),
            P("section"),
            P("section", None, None),
            P("section", None),
            P("section", None, None),
        ),
        out_specs=P("section", None, "coil", "cuts", None, None),
        check_vma=False,
    )
```

time: 531 us -> 89.2 us (0.17)
  the two profiles are of different devices: /device:TPU:6 before, /device:TPU:39 now
where the time goes in v1:
time: 89.2 us; the launch traced here: 88.7 us
  Pallas kernels  74.8 us (84%)
  local copies, waits for them, and re-layouts  13.2 us (15%)
    pallas_call x1, Pallas kernels, body(): pl.pallas_call(kernel, out_shape=jax.ShapeDtypeStruct((slabs, SIZE_Y, SIZ...  74.8 us
    unnamed x26, local copies, waits for them, and re-layouts  13.2 us

profile of v1, /device:TPU:39, one launch (start us, length us, event | category | flops | bytes accessed | tf_op | source)
XLA Modules:
  0.0 88.7 jit_solution(10494398011758463933)
XLA Ops:
  0.7 0.8 copy.15.conv_in
  1.5 0.0 copy-start
  1.5 1.7 %copy-done = bf16[2,1,32,80,2,128]{5,4,3,2,1,0:T(2,128)(2,1)S(1)} copy-done((bf16[2,1,32,80,2,128]{5,4,3,2,1,0:T(2,128)(2,1)S(1)}, bf16[2,1,32,80,2,128]{5,4,3,2,1,0:T(2,128)(2,1)}, u32[]{:S(2)}) %copy-start) | copy-done | bytes 2621464
  3.2 0.0 copy-start.1
  3.2 1.7 %copy-done.1 = bf16[2,1,32,80,2,128]{5,4,3,2,1,0:T(2,128)(2,1)S(1)} copy-done((bf16[2,1,32,80,2,128]{5,4,3,2,1,0:T(2,128)(2,1)S(1)}, bf16[2,1,32,80,2,128]{5,4,3,2,1,0:T(2,128)(2,1)}, u32[]{:S(2)}) %copy-start.1) | copy-done | bytes 2621464
  5.0 0.0 copy-start.2
  5.0 1.0 %copy-done.2 = bf16[800,160]{1,0:T(8,128)(2,1)S(1)} copy-done((bf16[800,160]{1,0:T(8,128)(2,1)S(1)}, bf16[800,160]{1,0:T(8,128)(2,1)}, u32[]{:S(2)}) %copy-start.2) | copy-done | bytes 256024
  6.0 0.0 copy-start.3
  6.0 1.0 %copy-done.3 = bf16[640,176]{1,0:T(8,128)(2,1)S(1)} copy-done((bf16[640,176]{1,0:T(8,128)(2,1)S(1)}, bf16[640,176]{1,0:T(8,128)(2,1)}, u32[]{:S(2)}) %copy-start.3) | copy-done | bytes 225304
  6.9 0.0 copy-start.4
  6.9 0.9 %copy-done.4 = bf16[512,256]{1,0:T(8,128)(2,1)S(1)} copy-done((bf16[512,256]{1,0:T(8,128)(2,1)S(1)}, bf16[512,256]{1,0:T(8,128)(2,1)}, u32[]{:S(2)}) %copy-start.4) | copy-done | bytes 262168
  7.9 0.0 copy-start.5
  7.9 0.9 %copy-done.5 = bf16[160,640]{1,0:T(8,128)(2,1)S(1)} copy-done((bf16[160,640]{1,0:T(8,128)(2,1)S(1)}, bf16[160,640]{1,0:T(8,128)(2,1)}, u32[]{:S(2)}) %copy-start.5) | copy-done | bytes 204824
  8.8 0.0 copy-start.6
  8.8 0.9 copy-done.6
  9.7 0.0 copy-start.7
  9.7 0.8 copy-done.7
  10.5 0.0 copy-start.8
  10.5 0.7 copy-done.8
  11.2 0.0 copy-start.9
  11.2 0.7 copy-done.9
  11.9 0.0 copy-start.10
  11.9 0.7 copy-done.10
  12.6 0.0 copy-start.11
  12.6 0.7 copy-done.11
  13.2 74.8 %shard_map.136 = bf16[2,80,128]{2,1,0:T(8,128)(2,1)S(1)} custom-call(bf16[2,80,128]{2,1,0:T(8,128)(2,1)S(1)} %bitcast.9, bf16[2,32,160,128]{3,2,1,0:T(8,128)(2,1)S(1)} %bitcast.6, bf16[2,32,160,128]{3,2,1,0:T(8,128)(2,1)S(1)} %bitcast.7, s32[2,80,128]{2,1,0:T(8,128)S(1)} %copy-done.6, f32[1]{0:T(128)S(6)} %copy.18.step, ...), custom_call_target="tpu_custom_call" | custom-call | tf_op jit(solution)/shard_map/pallas_call | solution.py:537
  88.0 0.6 copy.19
Async XLA Ops:
  1.5 1.7 %copy-start = (bf16[2,1,32,80,2,128]{5,4,3,2,1,0:T(2,128)(2,1)S(1)}, bf16[2,1,32,80,2,128]{5,4,3,2,1,0:T(2,128)(2,1)}, u32[]{:S(2)}) copy-start(bf16[2,1,32,80,2,128]{5,4,3,2,1,0:T(2,128)(2,1)} %param.15) | copy-start | bytes 7864324
  3.2 1.7 %copy-start.1 = (bf16[2,1,32,80,2,128]{5,4,3,2,1,0:T(2,128)(2,1)S(1)}, bf16[2,1,32,80,2,128]{5,4,3,2,1,0:T(2,128)(2,1)}, u32[]{:S(2)}) copy-start(bf16[2,1,32,80,2,128]{5,4,3,2,1,0:T(2,128)(2,1)} %param.16) | copy-start | bytes 7864324
  5.0 1.0 %copy-start.2 = (bf16[800,160]{1,0:T(8,128)(2,1)S(1)}, bf16[800,160]{1,0:T(8,128)(2,1)}, u32[]{:S(2)}) copy-start(bf16[800,160]{1,0:T(8,128)(2,1)} %constant.12.clone.square_in) | copy-start | bytes 768004
  6.0 1.0 %copy-start.3 = (bf16[640,176]{1,0:T(8,128)(2,1)S(1)}, bf16[640,176]{1,0:T(8,128)(2,1)}, u32[]{:S(2)}) copy-start(bf16[640,176]{1,0:T(8,128)(2,1)} %constant.14.clone.taps_in) | copy-start | bytes 675844
  6.9 0.9 %copy-start.4 = (bf16[512,256]{1,0:T(8,128)(2,1)S(1)}, bf16[512,256]{1,0:T(8,128)(2,1)}, u32[]{:S(2)}) copy-start(bf16[512,256]{1,0:T(8,128)(2,1)} %constant.13.clone.wide_in) | copy-start | bytes 786436
  7.9 0.9 %copy-start.5 = (bf16[160,640]{1,0:T(8,128)(2,1)S(1)}, bf16[160,640]{1,0:T(8,128)(2,1)}, u32[]{:S(2)}) copy-start(bf16[160,640]{1,0:T(8,128)(2,1)} %constant.15.clone.gather_in) | copy-start | bytes 614404
  8.8 0.9 %copy-start.6 = (s32[2,80,128]{2,1,0:T(8,128)S(1)}, s32[2,80,128]{2,1,0:T(8,128)}, u32[]{:S(2)}) copy-start(s32[2,80,128]{2,1,0:T(8,128)} %mask.1) | copy-start | bytes 245764
  9.7 0.8 copy-start.7
  10.5 0.7 copy-start.8
  11.2 0.7 copy-start.9
  11.9 0.7 copy-start.10
  12.6 0.7 copy-start.11

commit v2 on v1

--- a/solution.py
+++ b/solution.py
@@ -47,16 +47,21 @@
                 for part in range(2):
                     taps[row * 8 + shift * 2 + part, part * SIZE_Y + other] = 1.0
                     gather[part * SIZE_Y + row, other * 8 + shift * 2 + part] = 1.0
-    place_in = np.zeros((18, 128))
-    place_out = np.zeros((32, 18))
+    place = np.zeros((32, ROWS))
     for shift_row in range(3):
         for shift_col in range(3):
             for part in range(2):
-                place = shift_col * 8 + shift_row * 2 + part
-                column = (3 * shift_row + shift_col) * 2 + part
-                place_in[column, place] = 1.0
-                place_out[place, column] = 1.0
-    return [part.astype(ml_dtypes.bfloat16) for part in (square, wide, taps, gather, place_in, place_out)]
+                place[shift_col * 8 + shift_row * 2 + part, (3 * shift_row + shift_col) * 2 + part] = 1.0
+    spread = np.zeros((32, 8 * 256))
+    fold = np.zeros((2 * 48, ROWS))
+    for shift_col in range(3):
+        for r in range(8):
+            for i in range(8):
+                spread[shift_col * 8 + r, i * 256 + shift_col * 64 + i * 8 + r] = 1.0
+            for i in range(2):
+                fold[i * 48 + shift_col * 16 + i * 8 + r, shift_col * 8 + r] = 1.0
+    square = np.concatenate([square, place, fold], axis=0)
+    return [part.astype(ml_dtypes.bfloat16) for part in (square, wide, taps, gather, spread)]
 
 
 def twiddles():
@@ -106,12 +111,12 @@
 
 def kernel(
     initial, sens, kspace, mask, step, conv_in, bias, conv_out,
-    square_in, wide_in, taps_in, gather_in, place_in, place_out,
+    square_in, wide_in, taps_in, gather_in, spread_in,
     out,
-    square, wide, taps_sel, gather_sel,
+    square, wide, taps_sel, gather_sel, spread, first_block, second_block, mask_here, conv_in_here, bias_here, conv_out_here,
     kbuf, ubuf, gbuf, tbuf, sown, bpart, brecv, bsum, bin_, btot,
     srecv, splan, ibuf, wbuf, fbuf, mplan, mwoven,
-    vbuf, wspec, partial, arrived, tapbuf, prodbuf, obuf,
+    vbuf, wspec, partial, arrived, tapbuf, hidbuf, prodbuf, obuf,
     local_sem, own_sem, s_send, s_recv, i_send, i_recv, w_send, w_recv,
     x_send, x_recv, b_send, b_recv, r_send, r_recv, o_send, o_recv,
 ):
@@ -141,7 +146,14 @@
         pltpu.make_async_copy(wide_in, wide, local_sem.at[2]),
         pltpu.make_async_copy(taps_in, taps_sel, local_sem.at[3]),
         pltpu.make_async_copy(gather_in, gather_sel, local_sem.at[4]),
+        pltpu.make_async_copy(mask.at[slab], mask_here, local_sem.at[5]),
+        pltpu.make_async_copy(conv_in, conv_in_here, local_sem.at[6]),
+        pltpu.make_async_copy(bias, bias_here, local_sem.at[7]),
+        pltpu.make_async_copy(conv_out, conv_out_here, local_sem.at[8]),
+        pltpu.make_async_copy(spread_in, spread, local_sem.at[10]),
     ]
+    half = pl.multiple_of(core * SIZE_Y, SIZE_Y)
+    own_half = pltpu.make_async_copy(initial.at[slab], ibuf.at[pl.ds(half, SIZE_Y)], local_sem.at[9])
     own_loads = []
     for slot in range(SLOTS):
         _, position, _ = toward(slot // 4, slot % 4)
@@ -164,7 +176,6 @@
             src_ref=src, dst_ref=dst, send_sem=send, recv_sem=recv, device_id=device, device_id_type=MESH
         )
 
-    half = pl.multiple_of(core * SIZE_Y, SIZE_Y)
     image_copies = [
         remote(initial.at[slab], ibuf.at[pl.ds(half, SIZE_Y)], i_send.at[k], i_recv.at[core], mates[k])
         for k in range(3)
@@ -174,7 +185,7 @@
     def _():
         for copy in image_copies:
             copy.start()
-        ibuf[pl.ds(half, SIZE_Y)] = initial[slab]
+        own_half.start()
 
     sens_copies = []
     for slot in range(1, SLOTS):
@@ -185,15 +196,19 @@
     for copy in sens_copies:
         copy.start()
 
-    bias_rows = jnp.broadcast_to(bias[...], (128, 128))
+    for load in (loads[0], loads[6], loads[7], loads[8]):
+        load.wait()
+    bias_rows = jnp.broadcast_to(bias_here[...], (32, 128))
     high = bias_rows.astype(BF).astype(F32)
     middle = (bias_rows - high).astype(BF).astype(F32)
     low = bias_rows - high - middle
-    which = lax.broadcasted_iota(jnp.int32, (128, 128), 0)
+    which = lax.broadcasted_iota(jnp.int32, (32, 128), 0)
     stacked = jnp.where(which == 6, high, jnp.where(which == 14, middle, jnp.where(which == 22, low, 0.0)))
-    first_layer = dot(conv_in[0], place_in[...]) + stacked.T
-    wbuf[sec, 0:128] = (0.5 * first_layer).astype(BF)
-    wbuf[sec, 128:160] = dot(place_out[...], conv_out[0]).astype(BF)
+    place = square[5 * ROWS : 5 * ROWS + 32][:, 0:18]
+    first_layer = dot(place, conv_in_here[0]) + stacked
+    first_layer = jnp.concatenate([0.5 * first_layer, jnp.zeros((96, 128), F32)], axis=0)
+    wbuf[sec, 0:128] = first_layer.T.astype(BF)
+    wbuf[sec, 128:160] = dot(place, conv_out_here[0]).astype(BF)
     fbuf[sec] = jnp.full((8, 128), step[0], F32)
     net_copies = []
     for k in range(3):
@@ -202,8 +217,8 @@
     for copy in net_copies:
         copy.start()
 
-    loads[0].wait()
-    plane = mask[slab].astype(F32).astype(BF)
+    loads[5].wait()
+    plane = mask_here[...].astype(F32).astype(BF)
     both = jnp.concatenate([plane, plane], axis=0)
     mplan[...] = jnp.concatenate([both, both], axis=1)
     mwoven[...] = dot(square[4 * ROWS : 5 * ROWS], both).astype(BF)
@@ -313,7 +328,32 @@
     def _():
         arrival(1).wait_recv()
 
+    @pl.when(home)
+    def _():
+        own_half.wait()
+
     image = by_lanes(dot(square[3 * ROWS : 4 * ROWS], ibuf[...]))
+
+    def net_arrival(c, buf, index):
+        return remote(buf.at[c], buf.at[c], w_send.at[0], w_recv.at[index], others[0])
+
+    for k in range(3):
+        other = (sec + k + 1) % 4
+        net_arrival(other, wbuf, other).wait_recv()
+        net_arrival(other, fbuf, 4 + other).wait_recv()
+
+    loads[9].wait()
+
+    def blocks(c, _):
+        layer = wbuf[c, 0:128][:, 0:32]
+        for i in range(8):
+            first_block[c, i * 128 : (i + 1) * 128] = dot(layer, spread[:, i * 256 : (i + 1) * 256]).astype(BF)
+        for i in range(2):
+            rows = square[5 * ROWS + 32 + 48 * i : 5 * ROWS + 80 + 48 * i][:, 0:32]
+            second_block[c, :, i * 128 : (i + 1) * 128] = dot(rows, wbuf[c, 128:160]).astype(BF)
+        return 0
+
+    lax.fori_loop(0, CASCADES, blocks, 0)
 
     for k in range(8):
         if k:
@@ -332,14 +372,6 @@
 
     def moved_left(x):
         return jnp.where(lane == SIZE_Z - 1, 0.0, pltpu.roll(x, SIZE_Z - 1, 1))
-
-    def net_arrival(c, buf, index):
-        return remote(buf.at[c], buf.at[c], w_send.at[0], w_recv.at[index], others[0])
-
-    for k in range(3):
-        other = (sec + k + 1) % 4
-        net_arrival(other, wbuf, other).wait_recv()
-        net_arrival(other, fbuf, 4 + other).wait_recv()
 
     def operator(image):
         real, imag = image[:, :SIZE_Z], image[:, SIZE_Z:]
@@ -371,29 +403,28 @@
         three = jnp.concatenate([moved_right(planar), planar, moved_left(planar)], axis=1)
         lift = jnp.where(lax.broadcasted_iota(jnp.int32, (16, 3 * SIZE_Z), 0) == 0, 1.0, 0.0)
         operand = jnp.concatenate([three, lift], axis=0).astype(BF)
-        tapbuf[...] = dot(taps_sel[...], operand)
-        zero = jnp.zeros((8, SIZE_Z), F32)
-
-        def rows_of(step_index, _):
-            for i in range(4):
-                base = pl.multiple_of(step_index * 64 + i * 16, 16)
-                eight = [tapbuf[pl.ds(base + 8 * k, 8)] for k in range(2)]
-                columns = [
-                    jnp.concatenate([e[:, 0:128], e[:, 128:256], e[:, 256:384], zero], axis=0) for e in eight
-                ]
-                near = jnp.concatenate(columns, axis=1).astype(BF)
-                pre = dot(wbuf[c, 0:128][:, 0:32], near)
-                hidden = (pre + pre * jnp.tanh(pre)).astype(BF)
-                product = dot(wbuf[c, 128:160], hidden)
+        tapbuf[...] = dot(taps_sel[...], operand).astype(BF)
+        for g in range(5):
+            near = [
+                jnp.concatenate(
+                    [tapbuf[128 * g + 64 * k : 128 * g + 64 * (k + 1), d * 128 : (d + 1) * 128] for d in range(3)], axis=0
+                )
+                for k in range(2)
+            ]
+            near = jnp.concatenate(near, axis=1)
+            for t in range(4):
+                pre = dot(first_block[c, t * 256 : (t + 1) * 256][:, 0:192], near).astype(BF)
+                hidbuf[g * 4 + t] = pre + pre * jnp.tanh(pre)
+        for g in range(5):
+            for t in range(4):
+                product = dot(second_block[c], hidbuf[g * 4 + t]).astype(BF)
                 for k in range(2):
+                    top = 128 * g + 64 * k + 16 * t
                     for d in range(3):
-                        prodbuf[pl.ds(base + 8 * k, 8), d * 128 : (d + 1) * 128] = product[
-                            d * 8 : (d + 1) * 8, k * 128 : (k + 1) * 128
+                        prodbuf[top : top + 16, d * 128 : (d + 1) * 128] = product[
+                            d * 16 : (d + 1) * 16, k * 128 : (k + 1) * 128
                         ]
-            return 0
-
-        lax.fori_loop(0, 10, rows_of, 0)
-        summed = dot(gather_sel[...], prodbuf[...].astype(BF))
+        summed = dot(gather_sel[...], prodbuf[...])
         total = moved_right(summed[:, 0:128]) + summed[:, 128:256] + moved_left(summed[:, 256:384])
         return by_lanes(total)
 
@@ -482,6 +513,7 @@
     initial = initial.reshape(slabs, SIZE_Y, SIZE_Z)
     sens = sens.reshape(slabs, SIZE_X, ROWS, SIZE_Z)
     kspace = kspace.reshape(slabs, SIZE_X, ROWS, SIZE_Z)
+    conv_in = jnp.swapaxes(conv_in, 1, 2)
     tables = [jnp.asarray(part) for part in constants()]
     vmem = pl.BlockSpec(memory_space=pltpu.VMEM)
     hbm = pl.BlockSpec(memory_space=pltpu.HBM)
@@ -489,10 +521,17 @@
     dma = pltpu.SemaphoreType.DMA
     slice_shape = (SIZE_Y, 2 * SIZE_Z)
     scratch = [
-        pltpu.VMEM((5 * ROWS, ROWS), BF),
+        pltpu.VMEM((5 * ROWS + 128, ROWS), BF),
         pltpu.VMEM((512, 256), BF),
         pltpu.VMEM((SIZE_Y * 8, ROWS + 16), BF),
         pltpu.VMEM((ROWS, SIZE_Y * 8), BF),
+        pltpu.VMEM((32, 8 * 256), BF),
+        pltpu.VMEM((CASCADES, 8 * HID, 256), BF),
+        pltpu.VMEM((CASCADES, 48, 2 * HID), BF),
+        pltpu.VMEM((SIZE_Y, SIZE_Z), jnp.int32),
+        pltpu.VMEM((1, 18, HID), BF),
+        pltpu.VMEM((1, HID), F32),
+        pltpu.VMEM((1, 18, HID), BF),
         pltpu.VMEM((SIZE_X, ROWS, SIZE_Z), BF),
         pltpu.VMEM((16, ROWS, SIZE_Z), F32),
         pltpu.VMEM((16, 32, SIZE_Z), F32),
@@ -514,10 +553,11 @@
         pltpu.VMEM((SLOTS * SIZE_Y, 2 * SIZE_Z), BF),
         pltpu.VMEM((CASCADES, *slice_shape), BF),
         pltpu.VMEM((CASCADES, 3, *slice_shape), BF),
-        pltpu.VMEM((SIZE_Y * 8, 3 * SIZE_Z), F32),
-        pltpu.VMEM((SIZE_Y * 8, 3 * SIZE_Z), F32),
+        pltpu.VMEM((SIZE_Y * 8, 3 * SIZE_Z), BF),
+        pltpu.VMEM((20, 256, 256), BF),
+        pltpu.VMEM((SIZE_Y * 8, 3 * SIZE_Z), BF),
         pltpu.VMEM((CASCADES, SIZE_Y, SIZE_Z), BF),
-        dma((5,)),
+        dma((11,)),
         dma((SLOTS,)),
         dma((SLOTS,)),
         dma((SLOTS,)),
@@ -537,11 +577,11 @@
     result = pl.pallas_call(
         kernel,
         out_shape=jax.ShapeDtypeStruct((slabs, SIZE_Y, SIZE_Z), BF),
-        in_specs=[vmem, hbm, hbm, vmem, smem, vmem, vmem, vmem, hbm, hbm, hbm, hbm, vmem, vmem],
+        in_specs=[hbm] * 4 + [smem] + [hbm] * 8,
         out_specs=vmem,
         scratch_shapes=scratch,
         compiler_params=pltpu.CompilerParams(
-            collective_id=0, has_side_effects=True, vmem_limit_bytes=40 << 20
+            collective_id=0, has_side_effects=True, vmem_limit_bytes=62 << 20
         ),
     )(initial, sens, kspace, mask, step_sizes, conv_in, bias_in, conv_out, *tables)
     return result.reshape(1, slabs, 1, SIZE_Y // 2, 2, SIZE_Z)

time: 89.2 us -> 55.4 us (0.62)
  the two profiles are of different devices: /device:TPU:39 before, /device:TPU:6 now
where the time goes in v2:
time: 55.4 us; the launch traced here: 55 us
  Pallas kernels  53 us (96%)
  local copies, waits for them, and re-layouts  1.43 us (3%)
  between operations  0.66 us (1%)
    pallas_call x1, Pallas kernels, body(): pl.pallas_call(kernel, out_shape=jax.ShapeDtypeStruct((slabs, SIZE_Y, SIZ...  53 us
    unnamed x1, local copies, waits for them, and re-layouts  1.43 us

profile of v2, /device:TPU:6, one launch (start us, length us, event | category | flops | bytes accessed | tf_op | source)
XLA Modules:
  0.0 55.0 jit_solution(14625303346319262288)
XLA Ops:
  0.7 53.0 %shard_map.127 = bf16[2,80,128]{2,1,0:T(8,128)(2,1)} custom-call(bf16[2,80,128]{2,1,0:T(8,128)(2,1)} %bitcast.10, bf16[2,32,160,128]{3,2,1,0:T(8,128)(2,1)} %bitcast.7, bf16[2,32,160,128]{3,2,1,0:T(8,128)(2,1)} %bitcast.8, s32[2,80,128]{2,1,0:T(8,128)} %mask.1, f32[1]{0:T(128)S(6)} %copy.16.step, bf16[1,18,128]{2,1,0:T(8,128)(2,1)} %bitcast.11, ...), custom_call_target="tpu_custom_call" | custom-call | tf_op jit(solution)/shard_map/pallas_call | solution.py:577
  53.6 1.4 %copy.17 = bf16[1,2,1,40,2,128]{5,4,3,2,1,0:T(2,128)(2,1)} copy(bf16[1,2,1,40,2,128]{5,4,3,2,1,0:T(2,128)(2,1)} %bitcast.9) | data formatting | bytes 81920

commit v3 on v2

--- a/solution.py
+++ b/solution.py
@@ -114,16 +114,16 @@
     square_in, wide_in, taps_in, gather_in, spread_in,
     out,
     square, wide, taps_sel, gather_sel, spread, first_block, second_block, mask_here, conv_in_here, bias_here, conv_out_here,
-    kbuf, ubuf, gbuf, tbuf, sown, bpart, brecv, bsum, bin_, btot,
+    kbuf, ubuf, gbuf, tbuf, sown, bpart, brecv, bsum, yrecv, zsum, bin_, btot,
     srecv, splan, ibuf, wbuf, fbuf, mplan, mwoven,
     vbuf, wspec, partial, arrived, tapbuf, hidbuf, prodbuf, obuf,
     local_sem, own_sem, s_send, s_recv, i_send, i_recv, w_send, w_recv,
-    x_send, x_recv, b_send, b_recv, r_send, r_recv, o_send, o_recv,
+    x_send, x_recv, y_send, y_recv, b_send, b_recv, r_send, r_recv, o_send, o_recv,
 ):
     sec, pos, core = lax.axis_index("section"), lax.axis_index("coil"), lax.axis_index("cuts")
     row, col = pos // 8, pos % 8
     odd_col = col % 2
-    sign = 1 - 2 * odd_col
+    sign = 1 - 2 * ((col + row) % 2)
     odd = sec % 2
     slab = sec // 2
     home = odd_col == odd
@@ -131,14 +131,21 @@
     def at(section, y, z, c):
         return (section, y * 8 + z, c)
 
-    twin = col + sign
+    twin = (col + sign + 8) % 8
     mates = [at(sec, row, col, 1 - core), at(sec, row, twin, core), at(sec, row, twin, 1 - core)]
     others = [((sec + k) % 4, pos, core) for k in (1, 2, 3)]
 
     def toward(j, dy):
-        z = (col + (1 - 2 * (j % 2)) * sign * j + 8) % 8
+        z = (col + (1 - 2 * (j % 2)) * (1 - 2 * (dy % 2)) * sign * j + 8) % 8
         y = (row + dy) % 4
-        return at(sec, y, z, core), 8 * y + 2 * (z // 2) + odd, y * 4 + z // 2
+        pair = (z + 1 - 2 * ((z + y) % 2) + 8) % 8
+        held = jnp.where(z % 2 == odd, z, pair)
+        return at(sec, y, z, core), 8 * y + held, y * 4 + held // 2
+
+    barrier = pltpu.get_barrier_semaphore()
+    greet = [at(sec, (row + dy) % 4, (col - sign * j + 8) % 8, core) for j in (3, 2, 1, 0) for dy in (2, 1, 3, 0)][:-1]
+    for device in greet + others + mates:
+        pl.semaphore_signal(barrier, inc=1, device_id=device, device_id_type=MESH)
 
     loads = [
         pltpu.make_async_copy(square_in, square, local_sem.at[0]),
@@ -161,20 +168,31 @@
     for load in loads + own_loads:
         load.start()
 
-    barrier = pltpu.get_barrier_semaphore()
-    greet = list(mates) + list(others)
-    for offset in (0, 2, -1, -3, -2):
-        for dy in range(4):
-            if offset or dy:
-                greet.append(at(sec, (row + dy) % 4, (col + sign * offset + 8) % 8, core))
-    for device in greet:
-        pl.semaphore_signal(barrier, inc=1, device_id=device, device_id_type=MESH)
-    pl.semaphore_wait(barrier, len(greet))
-
     def remote(src, dst, send, recv, device):
         return pltpu.make_async_remote_copy(
             src_ref=src, dst_ref=dst, send_sem=send, recv_sem=recv, device_id=device, device_id_type=MESH
         )
+
+    for load in (loads[0], loads[5]):
+        load.wait()
+    plane = mask_here[...].astype(F32).astype(BF)
+    both = jnp.concatenate([plane, plane], axis=0)
+    mplan[...] = jnp.concatenate([both, both], axis=1)
+    mwoven[...] = dot(square[4 * ROWS : 5 * ROWS], both).astype(BF)
+    loads[1].wait()
+
+    fold = (1 - 2 * odd).astype(F32)
+
+    def data_rows(n, _):
+        masked = mwoven[...]
+        two = jnp.concatenate([kbuf[n] * masked, kbuf[n + 16] * masked], axis=1)
+        done = dot(square[0:ROWS], two)
+        ubuf[n] = done[:, :SIZE_Z] + fold * done[:, SIZE_Z:]
+        return 0
+
+    lax.fori_loop(0, 16, data_rows, 0, unroll=4)
+
+    pl.semaphore_wait(barrier, len(greet) + 6)
 
     image_copies = [
         remote(initial.at[slab], ibuf.at[pl.ds(half, SIZE_Y)], i_send.at[k], i_recv.at[core], mates[k])
@@ -196,7 +214,79 @@
     for copy in sens_copies:
         copy.start()
 
-    for load in (loads[0], loads[6], loads[7], loads[8]):
+    first, second = twiddles()
+
+    def coefficient(table):
+        even_value, odd_value = complex(table[0]), complex(table[1])
+        return (
+            jnp.where(odd == 0, np.float32(even_value.real), np.float32(odd_value.real)),
+            jnp.where(odd == 0, np.float32(even_value.imag), np.float32(odd_value.imag)),
+        )
+
+    def weighted(terms):
+        real, imag = None, None
+        for (w_real, w_imag), (v_real, v_imag) in terms:
+            r = w_real * v_real - w_imag * v_imag
+            i = w_real * v_imag + w_imag * v_real
+            real, imag = (r, i) if real is None else (real + r, imag + i)
+        return real, imag
+
+    def x_pass(chunk, _):
+        top = pl.multiple_of(chunk * 16, 16)
+        below = pl.multiple_of(SIZE_Y + chunk * 16, 16)
+        for n in range(4):
+            u = [(ubuf[n + 4 * k, pl.ds(top, 16)], ubuf[n + 4 * k, pl.ds(below, 16)]) for k in range(4)]
+            for a in range(4):
+                real, imag = weighted([(coefficient(first[:, k, a]), u[k]) for k in range(4)])
+                gbuf[n * 4 + a, 0:16] = real
+                gbuf[n * 4 + a, 16:32] = imag
+        for a in range(4):
+            g = [(gbuf[n * 4 + a, 0:16], gbuf[n * 4 + a, 16:32]) for n in range(4)]
+            for b in range(4):
+                real, imag = weighted([(coefficient(second[:, n, b, a]), g[n]) for n in range(4)])
+                tbuf[b * 4 + a, pl.ds(top, 16), 0:SIZE_Z] = real.astype(BF)
+                tbuf[b * 4 + a, pl.ds(top, 16), SIZE_Z:] = imag.astype(BF)
+        return 0
+
+    lax.fori_loop(0, 5, x_pass, 0)
+    loads[2].wait()
+    for load in own_loads:
+        load.wait()
+
+    def share(parity):
+        def one(q, _):
+            jh = q // 2
+            j = 2 * jh + parity
+            dy = 2 * (q % 2)
+            _, _, e0 = toward(j, dy)
+            _, _, e1 = toward(j, dy + 1)
+            done = dot(jnp.concatenate([tbuf[e0], tbuf[e1]], axis=0), wide[256:512])
+            slot = j * 4 + dy
+            pair = dot(square[3 * ROWS : 4 * ROWS], jnp.concatenate([sown[slot], sown[slot + 1]], axis=1))
+            pair = swap_pair(pair)
+            for k in range(2):
+                real, imag = conj_times(pair[k * SIZE_Y : (k + 1) * SIZE_Y], done[k * SIZE_Y : (k + 1) * SIZE_Y])
+                bpart[parity, (dy + k) * 2 + jh] = jnp.concatenate([real, imag], axis=1).astype(BF)
+            return 0
+
+        lax.fori_loop(0, 4, one, 0, unroll=4)
+
+    share(1 - core)
+    exchange = remote(bpart.at[1 - core], brecv, x_send, x_recv, mates[0])
+    exchange.start()
+    share(core)
+    exchange.wait_recv()
+
+    for q in range(8):
+        bsum[q] = (bpart[core, q].astype(F32) + brecv[q].astype(F32)).astype(BF)
+    row_copies = [
+        remote(bsum.at[pl.ds(2 * dy, 2)], yrecv.at[dy], y_send.at[dy], y_recv.at[dy], at(sec, (row + dy) % 4, col, core))
+        for dy in (1, 2, 3)
+    ]
+    for copy in row_copies:
+        copy.start()
+
+    for load in (loads[6], loads[7], loads[8]):
         load.wait()
     bias_rows = jnp.broadcast_to(bias_here[...], (32, 128))
     high = bias_rows.astype(BF).astype(F32)
@@ -217,105 +307,6 @@
     for copy in net_copies:
         copy.start()
 
-    loads[5].wait()
-    plane = mask_here[...].astype(F32).astype(BF)
-    both = jnp.concatenate([plane, plane], axis=0)
-    mplan[...] = jnp.concatenate([both, both], axis=1)
-    mwoven[...] = dot(square[4 * ROWS : 5 * ROWS], both).astype(BF)
-    loads[1].wait()
-
-    fold = (1 - 2 * odd).astype(F32)
-
-    def data_rows(n, _):
-        masked = mwoven[...]
-        two = jnp.concatenate([kbuf[n] * masked, kbuf[n + 16] * masked], axis=1)
-        done = dot(square[0:ROWS], two)
-        ubuf[n] = done[:, :SIZE_Z] + fold * done[:, SIZE_Z:]
-        return 0
-
-    lax.fori_loop(0, 16, data_rows, 0)
-
-    first, second = twiddles()
-
-    def coefficient(table):
-        even_value, odd_value = complex(table[0]), complex(table[1])
-        return (
-            jnp.where(odd == 0, np.float32(even_value.real), np.float32(odd_value.real)),
-            jnp.where(odd == 0, np.float32(even_value.imag), np.float32(odd_value.imag)),
-        )
-
-    def weighted(terms):
-        real, imag = None, None
-        for (w_real, w_imag), (v_real, v_imag) in terms:
-            r = w_real * v_real - w_imag * v_imag
-            i = w_real * v_imag + w_imag * v_real
-            real, imag = (r, i) if real is None else (real + r, imag + i)
-        return real, imag
-
-    def x_pass(chunk, _):
-        top = pl.multiple_of(chunk * 16, 16)
-        below = pl.multiple_of(SIZE_Y + chunk * 16, 16)
-        for n in range(4):
-            u = [(ubuf[n + 4 * k, pl.ds(top, 16)], ubuf[n + 4 * k, pl.ds(below, 16)]) for k in range(4)]
-            for a in range(4):
-                real, imag = weighted([(coefficient(first[:, k, a]), u[k]) for k in range(4)])
-                gbuf[n * 4 + a, 0:16] = real
-                gbuf[n * 4 + a, 16:32] = imag
-        for a in range(4):
-            g = [(gbuf[n * 4 + a, 0:16], gbuf[n * 4 + a, 16:32]) for n in range(4)]
-            for b in range(4):
-                real, imag = weighted([(coefficient(second[:, n, b, a]), g[n]) for n in range(4)])
-                tbuf[b * 4 + a, pl.ds(top, 16), 0:SIZE_Z] = real.astype(BF)
-                tbuf[b * 4 + a, pl.ds(top, 16), SIZE_Z:] = imag.astype(BF)
-        return 0
-
-    lax.fori_loop(0, 5, x_pass, 0)
-    loads[2].wait()
-    for load in own_loads:
-        load.wait()
-
-    def share(parity):
-        def one(q, _):
-            jh = q // 2
-            j = 2 * jh + parity
-            dy = 2 * (q % 2)
-            _, _, e0 = toward(j, dy)
-            _, _, e1 = toward(j, dy + 1)
-            done = dot(jnp.concatenate([tbuf[e0], tbuf[e1]], axis=0), wide[256:512])
-            slot = j * 4 + dy
-            pair = dot(square[3 * ROWS : 4 * ROWS], jnp.concatenate([sown[slot], sown[slot + 1]], axis=1))
-            pair = swap_pair(pair)
-            for k in range(2):
-                real, imag = conj_times(pair[k * SIZE_Y : (k + 1) * SIZE_Y], done[k * SIZE_Y : (k + 1) * SIZE_Y])
-                bpart[parity, jh * 4 + dy + k] = jnp.concatenate([real, imag], axis=1).astype(BF)
-            return 0
-
-        lax.fori_loop(0, 4, one, 0)
-
-    share(1 - core)
-    exchange = remote(bpart.at[1 - core], brecv, x_send, x_recv, mates[0])
-    exchange.start()
-    share(core)
-    exchange.wait_recv()
-
-    for q in range(8):
-        bsum[q] = (bpart[core, q].astype(F32) + brecv[q].astype(F32)).astype(BF)
-    data_copies = []
-    for q in range(8):
-        device, _, _ = toward(2 * (q // 4) + core, q % 4)
-        data_copies.append(remote(bsum.at[q], bin_.at[q], b_send.at[q], b_recv.at[q], device))
-
-    @pl.when(core == 0)
-    def _():
-        bin_[0] = bsum[0]
-
-    @pl.when(core == 1)
-    def _():
-        data_copies[0].start()
-
-    for copy in data_copies[1:]:
-        copy.start()
-
     def arrival(index):
         return remote(ibuf.at[pl.ds(index * SIZE_Y, SIZE_Y)], ibuf.at[pl.ds(index * SIZE_Y, SIZE_Y)],
                       i_send.at[0], i_recv.at[index], mates[0])
@@ -354,6 +345,26 @@
         return 0
 
     lax.fori_loop(0, CASCADES, blocks, 0)
+
+    for copy in row_copies:
+        copy.wait_recv()
+    for jh in range(2):
+        total = bsum[jh].astype(F32)
+        for dy in range(1, 4):
+            total = total + yrecv[dy, jh].astype(F32)
+        zsum[jh] = total.astype(BF)
+    data_copies = [
+        remote(zsum.at[jh], bin_.at[jh], b_send.at[jh], b_recv.at[jh], toward(2 * jh + core, 0)[0]) for jh in range(2)
+    ]
+    data_copies[1].start()
+
+    @pl.when(core == 0)
+    def _():
+        bin_[0] = zsum[0]
+
+    @pl.when(core == 1)
+    def _():
+        data_copies[0].start()
 
     for k in range(8):
         if k:
@@ -429,7 +440,7 @@
         return by_lanes(total)
 
     def data_arrival(q):
-        return remote(bsum.at[q], bin_.at[q], b_send.at[q], b_recv.at[q], mates[0])
+        return remote(zsum.at[q], bin_.at[q], b_send.at[q], b_recv.at[q], mates[0])
 
     def out_copy(c):
         return remote(obuf.at[c], out.at[slab], o_send.at[c], o_recv.at[slab], (c, pos, core))
@@ -443,12 +454,8 @@
             def _():
                 data_arrival(0).wait_recv()
 
-            for q in range(1, 8):
-                data_arrival(q).wait_recv()
-            total = bin_[0].astype(F32)
-            for q in range(1, 8):
-                total = total + bin_[q].astype(F32)
-            btot[...] = total
+            data_arrival(1).wait_recv()
+            btot[...] = bin_[0].astype(F32) + bin_[1].astype(F32)
 
         partial[c] = (sent - btot[...]).astype(BF)
         copies = [
@@ -500,7 +507,7 @@
         for copy in image_copies:
             copy.wait_send()
 
-    for copy in sens_copies + net_copies + [exchange] + data_copies[1:]:
+    for copy in sens_copies + net_copies + [exchange, data_copies[1]] + row_copies:
         copy.wait_send()
 
     @pl.when(core == 1)
@@ -540,7 +547,9 @@
         pltpu.VMEM((2, 8, *slice_shape), BF),
         pltpu.VMEM((8, *slice_shape), BF),
         pltpu.VMEM((8, *slice_shape), BF),
-        pltpu.VMEM((8, *slice_shape), BF),
+        pltpu.VMEM((4, 2, *slice_shape), BF),
+        pltpu.VMEM((2, *slice_shape), BF),
+        pltpu.VMEM((2, *slice_shape), BF),
         pltpu.VMEM(slice_shape, F32),
         pltpu.VMEM((SLOTS, ROWS, SIZE_Z), BF),
         pltpu.VMEM((SLOTS * SIZE_Y, 2 * SIZE_Z), BF),
@@ -567,8 +576,10 @@
         dma((8,)),
         dma,
         dma,
-        dma((8,)),
-        dma((8,)),
+        dma((4,)),
+        dma((4,)),
+        dma((2,)),
+        dma((2,)),
         dma((CASCADES, 3)),
         dma((CASCADES, 3)),
         dma((CASCADES,)),

time: 55.4 us -> 49.5 us (0.89)
  Pallas kernels: 53 us -> 47.2 us
    pallas_call x1, Pallas kernels: 53 us -> 47.2 us  [body(): pl.pallas_call(kernel, out_shape=jax.ShapeDtypeStruct((slabs, SIZE_Y, SIZ...]
where the time goes in v3:
time: 49.5 us; the launch traced here: 49.3 us
  Pallas kernels  47.2 us (95%)
  local copies, waits for them, and re-layouts  1.43 us (3%)
  between operations  0.66 us (1%)
    pallas_call x1, Pallas kernels, body(): pl.pallas_call(kernel, out_shape=jax.ShapeDtypeStruct((slabs, SIZE_Y, SIZ...  47.2 us
    unnamed x1, local copies, waits for them, and re-layouts  1.43 us

profile of v3, /device:TPU:6, one launch (start us, length us, event | category | flops | bytes accessed | tf_op | source)
XLA Modules:
  0.0 49.3 jit_solution(15093554488476629892)
XLA Ops:
  0.7 47.2 %shard_map.127 = bf16[2,80,128]{2,1,0:T(8,128)(2,1)} custom-call(bf16[2,80,128]{2,1,0:T(8,128)(2,1)} %bitcast.10, bf16[2,32,160,128]{3,2,1,0:T(8,128)(2,1)} %bitcast.7, bf16[2,32,160,128]{3,2,1,0:T(8,128)(2,1)} %bitcast.8, s32[2,80,128]{2,1,0:T(8,128)} %mask.1, f32[1]{0:T(128)S(6)} %copy.16.step, bf16[1,18,128]{2,1,0:T(8,128)(2,1)} %bitcast.11, ...), custom_call_target="tpu_custom_call" | custom-call | tf_op jit(solution)/shard_map/pallas_call | solution.py:588
  47.9 1.4 %copy.17 = bf16[1,2,1,40,2,128]{5,4,3,2,1,0:T(2,128)(2,1)} copy(bf16[1,2,1,40,2,128]{5,4,3,2,1,0:T(2,128)(2,1)} %bitcast.9) | data formatting | bytes 81920

commit v4 on v3

--- a/solution.py
+++ b/solution.py
@@ -587,7 +587,7 @@
     ]
     result = pl.pallas_call(
         kernel,
-        out_shape=jax.ShapeDtypeStruct((slabs, SIZE_Y, SIZE_Z), BF),
+        out_shape=pltpu.VMEM((slabs, SIZE_Y, SIZE_Z), BF),
         in_specs=[hbm] * 4 + [smem] + [hbm] * 8,
         out_specs=vmem,
         scratch_shapes=scratch,

time: 49.5 us -> 48 us (0.970)
  local copies, waits for them, and re-layouts: 1.43 us -> 0.62 us
  Pallas kernels: 47.2 us -> 46.6 us
    unnamed x1, local copies, waits for them, and re-layouts: 1.43 us -> 0.62 us
    pallas_call x1, Pallas kernels: 47.2 us -> 46.6 us  [body(): pl.pallas_call(kernel, out_shape=pltpu.VMEM((slabs, SIZE_Y, SIZE_Z), BF),...]
where the time goes in v4:
time: 48 us; the launch traced here: 47.9 us
  Pallas kernels  46.6 us (97%)
  between operations  0.66 us (1%)
  local copies, waits for them, and re-layouts  0.62 us (1%)
    pallas_call x1, Pallas kernels, body(): pl.pallas_call(kernel, out_shape=pltpu.VMEM((slabs, SIZE_Y, SIZE_Z), BF),...  46.6 us

profile of v4, /device:TPU:6, one launch (start us, length us, event | category | flops | bytes accessed | tf_op | source)
XLA Modules:
  0.0 47.9 jit_solution(9875533021050738985)
XLA Ops:
  0.7 46.6 %shard_map.127 = bf16[2,80,128]{2,1,0:T(8,128)(2,1)S(1)} custom-call(bf16[2,80,128]{2,1,0:T(8,128)(2,1)} %bitcast.10, bf16[2,32,160,128]{3,2,1,0:T(8,128)(2,1)} %bitcast.8, bf16[2,32,160,128]{3,2,1,0:T(8,128)(2,1)} %bitcast.9, s32[2,80,128]{2,1,0:T(8,128)} %mask.1, f32[1]{0:T(128)S(6)} %copy.17.step, bf16[1,18,128]{2,1,0:T(8,128)(2,1)} %bitcast.11, ...), custom_call_target="tpu_custom_call" | custom-call | tf_op jit(solution)/shard_map/pallas_call | solution.py:588
  47.3 0.6 %copy.16 = bf16[1,2,1,40,2,128]{5,4,3,2,1,0:T(2,128)(2,1)} copy(bf16[1,2,1,40,2,128]{5,4,3,2,1,0:T(2,128)(2,1)S(1)} %bitcast.7) | data formatting | bytes 81920

commit v5 on v4

--- a/solution.py
+++ b/solution.py
@@ -192,6 +192,7 @@
 
     lax.fori_loop(0, 16, data_rows, 0, unroll=4)
 
+    arrived[CASCADES - 1] = jnp.zeros((3, SIZE_Y, 2 * SIZE_Z), BF)
     pl.semaphore_wait(barrier, len(greet) + 6)
 
     image_copies = [
@@ -445,6 +446,14 @@
     def out_copy(c):
         return remote(obuf.at[c], out.at[slab], o_send.at[c], o_recv.at[slab], (c, pos, core))
 
+    def last_copy(k, for_core):
+        c, rows = CASCADES - 1, pl.ds(pl.multiple_of(32 * for_core, 16), 48)
+        return remote(
+            partial.at[c, rows], arrived.at[c, k, rows], r_send.at[c, k], r_recv.at[c, k], mates[k]
+        )
+
+    last_sends = [last_copy(0, 1 - core), last_copy(1, core), last_copy(2, 1 - core)]
+
     def cascade(c, image):
         sent = operator(image)
 
@@ -461,11 +470,28 @@
         copies = [
             remote(partial.at[c], arrived.at[c, k], r_send.at[c, k], r_recv.at[c, k], mates[k]) for k in range(3)
         ]
-        for copy in copies:
-            copy.start()
+        @pl.when(c < CASCADES - 1)
+        def _():
+            for copy in copies:
+                copy.start()
+
+        @pl.when(c == CASCADES - 1)
+        def _():
+            for copy in last_sends:
+                copy.start()
+
         refined = refine(image, c)
-        for copy in copies:
-            copy.wait_recv()
+
+        @pl.when(c < CASCADES - 1)
+        def _():
+            for copy in copies:
+                copy.wait_recv()
+
+        @pl.when(c == CASCADES - 1)
+        def _():
+            for k in range(3):
+                last_copy(k, core).wait_recv()
+
         total = partial[c].astype(F32)
         for k in range(3):
             total = total + arrived[c, k].astype(F32)
@@ -490,7 +516,10 @@
 
     for c in range(CASCADES):
         for k in range(3):
-            remote(partial.at[c], arrived.at[c, k], r_send.at[c, k], r_recv.at[c, k], mates[k]).wait_send()
+            if c < CASCADES - 1:
+                remote(partial.at[c], arrived.at[c, k], r_send.at[c, k], r_recv.at[c, k], mates[k]).wait_send()
+            else:
+                last_sends[k].wait_send()
 
         @pl.when(jnp.logical_and(home, c != sec))
         def _():

time: 48 us -> 47.4 us (0.987)
  Pallas kernels: 46.6 us -> 46 us
    pallas_call x1, Pallas kernels: 46.6 us -> 46 us  [body(): pl.pallas_call(kernel, out_shape=pltpu.VMEM((slabs, SIZE_Y, SIZE_Z), BF),...]
where the time goes in v5:
time: 47.4 us; the launch traced here: 47.3 us
  Pallas kernels  46 us (97%)
  between operations  0.66 us (1%)
  local copies, waits for them, and re-layouts  0.62 us (1%)
    pallas_call x1, Pallas kernels, body(): pl.pallas_call(kernel, out_shape=pltpu.VMEM((slabs, SIZE_Y, SIZE_Z), BF),...  46 us

profile of v5, /device:TPU:6, one launch (start us, length us, event | category | flops | bytes accessed | tf_op | source)
XLA Modules:
  0.0 47.3 jit_solution(16267611123757698288)
XLA Ops:
  0.7 46.0 %shard_map.127 = bf16[2,80,128]{2,1,0:T(8,128)(2,1)S(1)} custom-call(bf16[2,80,128]{2,1,0:T(8,128)(2,1)} %bitcast.10, bf16[2,32,160,128]{3,2,1,0:T(8,128)(2,1)} %bitcast.8, bf16[2,32,160,128]{3,2,1,0:T(8,128)(2,1)} %bitcast.9, s32[2,80,128]{2,1,0:T(8,128)} %mask.1, f32[1]{0:T(128)S(6)} %copy.17.step, bf16[1,18,128]{2,1,0:T(8,128)(2,1)} %bitcast.11, ...), custom_call_target="tpu_custom_call" | custom-call | tf_op jit(solution)/shard_map/pallas_call | solution.py:617
  46.7 0.6 %copy.16 = bf16[1,2,1,40,2,128]{5,4,3,2,1,0:T(2,128)(2,1)} copy(bf16[1,2,1,40,2,128]{5,4,3,2,1,0:T(2,128)(2,1)S(1)} %bitcast.7) | data formatting | bytes 81920

commit v6 on v5

--- a/solution.py
+++ b/solution.py
@@ -472,12 +472,12 @@
         ]
         @pl.when(c < CASCADES - 1)
         def _():
-            for copy in copies:
+            for copy in copies[::-1]:
                 copy.start()
 
         @pl.when(c == CASCADES - 1)
         def _():
-            for copy in last_sends:
+            for copy in last_sends[::-1]:
                 copy.start()
 
         refined = refine(image, c)

time: 47.4 us -> 48 us (1.013)
  Pallas kernels: 46 us -> 46.6 us
    pallas_call x1, Pallas kernels: 46 us -> 46.6 us  [body(): pl.pallas_call(kernel, out_shape=pltpu.VMEM((slabs, SIZE_Y, SIZE_Z), BF),...]
where the time goes in v6:
time: 48 us; the launch traced here: 47.9 us
  Pallas kernels  46.6 us (97%)
  between operations  0.66 us (1%)
  local copies, waits for them, and re-layouts  0.62 us (1%)
    pallas_call x1, Pallas kernels, body(): pl.pallas_call(kernel, out_shape=pltpu.VMEM((slabs, SIZE_Y, SIZE_Z), BF),...  46.6 us

profile of v6, /device:TPU:6, one launch (start us, length us, event | category | flops | bytes accessed | tf_op | source)
XLA Modules:
  0.0 47.9 jit_solution(9396721156962043167)
XLA Ops:
  0.7 46.6 %shard_map.127 = bf16[2,80,128]{2,1,0:T(8,128)(2,1)S(1)} custom-call(bf16[2,80,128]{2,1,0:T(8,128)(2,1)} %bitcast.10, bf16[2,32,160,128]{3,2,1,0:T(8,128)(2,1)} %bitcast.8, bf16[2,32,160,128]{3,2,1,0:T(8,128)(2,1)} %bitcast.9, s32[2,80,128]{2,1,0:T(8,128)} %mask.1, f32[1]{0:T(128)S(6)} %copy.17.step, bf16[1,18,128]{2,1,0:T(8,128)(2,1)} %bitcast.11, ...), custom_call_target="tpu_custom_call" | custom-call | tf_op jit(solution)/shard_map/pallas_call | solution.py:617
  47.3 0.6 %copy.16 = bf16[1,2,1,40,2,128]{5,4,3,2,1,0:T(2,128)(2,1)} copy(bf16[1,2,1,40,2,128]{5,4,3,2,1,0:T(2,128)(2,1)S(1)} %bitcast.7) | data formatting | bytes 81920
